TPU v7x, 32 devices: a whole 2x2x4 slice. The times are simulated.
32 devices in a mesh: pp: 4 (over x, core), ep: 8 (over z, y).
Axes of the slice: x: 2, y: 2, z: 4, core: 2. Of those that a mesh axis runs over, the one named last changes fastest.
Arguments:
- x_fwd: bfloat16 [4, 512, 7168], P('pp', 'ep'), may hold values from -6 to 6
- dy_bwd: bfloat16 [4, 512, 7168], P('pp', 'ep'), may hold values from -6 to 6
- routes_fwd: int32 [4, 512, 8], P('pp', 'ep'), may hold values from 0 to 255, as said below
- routes_bwd: int32 [4, 512, 8], P('pp', 'ep'), may hold values from 0 to 255, as said below
- score_fwd: float32 [4, 512, 8], P('pp', 'ep'), may hold values from 0.05 to 1
- score_bwd: float32 [4, 512, 8], P('pp', 'ep'), may hold values from 0.05 to 1
- saved_bwd: float32 [4, 8, 2, 2, 1024], P('pp', None, None, None, 'ep'), may hold values from -6 to 6
- w_gate: bfloat16 [7168, 1024], P(None, 'ep'), may hold values from -0.0625 to 0.0625
- w_up: bfloat16 [7168, 1024], P(None, 'ep'), may hold values from -0.0625 to 0.0625
- w_down: bfloat16 [1024, 7168], P('ep'), may hold values from -0.1875 to 0.1875
Outputs:
- received: bfloat16 [4, 512, 7168], P('pp', 'ep')
Inputs may be any that keep to these rules, and one draw needn't show every extreme that they name: `routes_fwd`: each token names 8 different ids. Within the 64 tokens of one block of a section, each expert below 1 is named at most 2 times, and in every section some expert below 1 is named exactly 2 times in every block. `routes_bwd`: the same as for routes_fwd.
All inputs are finite; a program needn't handle non-finite values.
Results may differ from a plain program's by a relative error of at most 0.008.
Values may be sent and summed in bfloat16 or wider, within the bound.
A program may use at most 64 MiB of HBM per device.

v0:
```python
import jax
import jax.numpy as jnp
from jax import lax
from jax.sharding import PartitionSpec as P

SPLIT = 8
CAP = 2


def shifted(value, axis, steps):
    count = lax.axis_size(axis)
    pairs = [(source, (source + steps) % count) for source in range(count)]
    return lax.ppermute(value, axis, pairs)


def route_tables(routes, scores, groups):
    experts = jnp.arange(groups, dtype=jnp.int32)
    match = (routes[:, :, None] == experts).astype(jnp.float32)
    weight = 2.5 * scores / jnp.sum(scores, axis=-1, keepdims=True)
    hits = jnp.sum(match, axis=1)
    shares = jnp.sum(match * weight[:, :, None], axis=1)
    before = jnp.cumsum(hits, axis=0) - hits
    slots = jnp.arange(CAP, dtype=jnp.float32)
    placed = hits[:, :, None] * (before[:, :, None] == slots).astype(jnp.float32)
    return (placed, placed * shares[:, :, None])


def dispatch(values, placed):
    groups = placed.shape[1]
    model_width = values.shape[1]
    buffer = jnp.einsum(
        "tgc,td->gcd", placed.astype(jnp.bfloat16), values, preferred_element_type=jnp.float32
    ).astype(jnp.bfloat16)
    outgoing = jnp.broadcast_to(buffer[:, None], (groups, SPLIT, CAP, model_width))
    outgoing = outgoing.reshape(groups * SPLIT, CAP, model_width)
    return lax.all_to_all(outgoing, "ep", split_axis=0, concat_axis=0, tiled=True)


def forward_partial(token_rows, w_gate, w_up, w_down):
    flat_rows = token_rows.reshape(-1, token_rows.shape[2])
    gate_pre = jnp.dot(flat_rows, w_gate, preferred_element_type=jnp.float32)
    up_pre = jnp.dot(flat_rows, w_up, preferred_element_type=jnp.float32)
    hidden = (jax.nn.silu(gate_pre) * up_pre).astype(jnp.bfloat16)
    partial_value = jnp.dot(hidden, w_down, preferred_element_type=jnp.float32).astype(jnp.bfloat16)
    return partial_value.reshape(token_rows.shape)


def backward_partial(token_rows, saved_rows, w_gate, w_up, w_down):
    contract = (((1,), (1,)), ((), ()))
    flat_rows = token_rows.reshape(-1, token_rows.shape[2])
    gate_saved = saved_rows[:, :, 0].reshape(-1, saved_rows.shape[3])
    up_saved = saved_rows[:, :, 1].reshape(-1, saved_rows.shape[3])
    grad_hidden = lax.dot_general(flat_rows, w_down, contract, preferred_element_type=jnp.float32)
    sigma = jax.nn.sigmoid(gate_saved)
    grad_gate = (grad_hidden * up_saved * sigma * (1.0 + gate_saved * (1.0 - sigma))).astype(
        jnp.bfloat16
    )
    grad_up = (grad_hidden * gate_saved * sigma).astype(jnp.bfloat16)
    partial_value = lax.dot_general(grad_gate, w_gate, contract, preferred_element_type=jnp.float32)
    partial_value = partial_value + lax.dot_general(
        grad_up, w_up, contract, preferred_element_type=jnp.float32
    )
    return partial_value.astype(jnp.bfloat16).reshape(token_rows.shape)


def combine(partial_value, weighted, groups):
    model_width = partial_value.shape[2]
    returned = lax.all_to_all(partial_value, "ep", split_axis=0, concat_axis=0, tiled=True)
    summed = jnp.sum(returned.reshape(groups, SPLIT, CAP, model_width).astype(jnp.float32), axis=1)
    mixed = jnp.einsum("tgc,gcd->td", weighted, summed, precision=lax.Precision.HIGHEST)
    return mixed.astype(jnp.bfloat16)


def body(
    x_fwd, dy_bwd, routes_fwd, routes_bwd, score_fwd, score_bwd, saved_bwd, w_gate, w_up, w_down
):
    groups = lax.axis_size("ep") // SPLIT
    placed_f, weighted_f = route_tables(routes_fwd[0], score_fwd[0], groups)
    rows_f = dispatch(x_fwd[0], placed_f)
    routed_f = combine(forward_partial(rows_f, w_gate, w_up, w_down), weighted_f, groups)
    placed_b, weighted_b = route_tables(routes_bwd[0], score_bwd[0], groups)
    rows_b = dispatch(dy_bwd[0], placed_b)
    routed_b = combine(
        backward_partial(rows_b, saved_bwd[0], w_gate, w_up, w_down), weighted_b, groups
    )
    from_before = shifted(routed_f, "pp", 1)
    from_after = shifted(routed_b, "pp", -1)
    total = from_before.astype(jnp.float32) + from_after.astype(jnp.float32)
    return total.astype(jnp.bfloat16)[None]


def solution(mesh):
    in_specs = (
        P("pp", "ep", None),
        P("pp", "ep", None),
        P("pp", "ep", None),
        P("pp", "ep", None),
        P("pp", "ep", None),
        P("pp", "ep", None),
        P("pp", None, None, None, "ep"),
        P(None, "ep"),
        P(None, "ep"),
        P("ep", None),
    )
    out_specs = P("pp", "ep", None)
    return jax.shard_map(body, mesh=mesh, in_specs=in_specs, out_specs=out_specs, check_vma=False)
```

profile of v0, /device:TPU:0, one launch (start us, length us, event | category | flops | bytes accessed | tf_op | source)
XLA Modules:
  0.0 77.8 jit_solution(10219225904643022618)
XLA Ops:
  0.0 0.9 %reduce_sum.77 = f32[64]{0:T(128)S(1)} reduce(f32[1,64,8]{1,2,0:T(8,128)} %param.15, f32[]{:T(128)} %constant.15.clone.1), dimensions={0,2}, to_apply=%region_7.8 | reduce | flops 448 | bytes 2308 | tf_op jit(solution)/shard_map/reduce_sum | solution.py:19
  0.9 0.7 fusion.29
  1.8 0.1 reduce.11
  1.9 1.4 %convolution_convert_fusion.3 = bf16[2,7168]{1,0:T(2,128)(2,1)S(1)} fusion(bf16[1,64,7168]{2,1,0:T(8,128)(2,1)} %param.11, f32[64]{0:T(128)S(1)} %get-tuple-element.8, f32[64]{0:T(128)S(1)} %sub.22), kind=kOutput, calls=%fused_computation.5 | convolution fusion | flops 1849600 | bytes 946688 | tf_op jit(solution)/shard_map/tgc,td->gcd/dot_general | solution.py:31
  3.3 0.8 %reshape.469 = bf16[8,2,7168]{2,1,0:T(2,128)(2,1)} broadcast(bf16[2,7168]{1,0:T(2,128)(2,1)S(1)} %convolution_convert_fusion.3), dimensions={1,2} | broadcast | bytes 258048 | tf_op jit(solution)/shard_map/reshape | solution.py:35
  4.1 7.3 %all-to-all-start.2 = ((bf16[8,2,7168]{2,1,0:T(2,128)(2,1)}), bf16[8,2,7168]{2,1,0:T(2,128)(2,1)S(1)}, u32[]{:S(2)}, u32[]{:S(2)}) async-start(bf16[8,2,7168]{2,1,0:T(2,128)(2,1)} %reshape.469), calls=%async_computation.2 | async-start | bytes 458752 | tf_op jit(solution)/shard_map/all_to_all | solution.py:36
  11.4 0.7 reduce_sum.73
  12.1 0.7 fusion.28
  13.0 0.1 reduce.10
  13.2 0.2 convolution_convert_fusion.4
  13.4 6.5 %all-to-all-done.2 = bf16[8,2,7168]{2,1,0:T(2,128)(2,1)S(1)} async-done(((bf16[8,2,7168]{2,1,0:T(2,128)(2,1)}), bf16[8,2,7168]{2,1,0:T(2,128)(2,1)S(1)}, u32[]{:S(2)}, u32[]{:S(2)}) %all-to-all-start.2) | async-done | bytes 229408 | tf_op jit(solution)/shard_map/all_to_all | solution.py:36
  19.9 0.8 %reshape.464 = bf16[8,2,7168]{2,1,0:T(2,128)(2,1)} broadcast(bf16[2,7168]{1,0:T(2,128)(2,1)S(1)} %convolution_convert_fusion.4), dimensions={1,2} | broadcast | bytes 258048 | tf_op jit(solution)/shard_map/reshape | solution.py:35
  20.7 3.4 %all-to-all-start = ((bf16[8,2,7168]{2,1,0:T(2,128)(2,1)}), bf16[8,2,7168]{2,1,0:T(2,128)(2,1)S(1)}, u32[]{:S(2)}, u32[]{:S(2)}) async-start(bf16[8,2,7168]{2,1,0:T(2,128)(2,1)} %reshape.464), calls=%async_computation | async-start | bytes 458752 | tf_op jit(solution)/shard_map/all_to_all | solution.py:36
  24.2 2.1 %fusion.51 = f32[16,128]{1,0:T(8,128)S(1)} fusion(bf16[16,7168]{1,0:T(8,128)(2,1)S(1)} %reshape.470, bf16[128,7168]{1,0:T(8,128)(2,1)} %param.19), kind=kOutput, calls=%fused_computation.72 | convolution fusion | flops 29360128 | bytes 2072576 | tf_op jit(solution)/shard_map/dot_general | solution.py:53
  26.3 5.9 %all-to-all-done = bf16[8,2,7168]{2,1,0:T(2,128)(2,1)S(1)} async-done(((bf16[8,2,7168]{2,1,0:T(2,128)(2,1)}), bf16[8,2,7168]{2,1,0:T(2,128)(2,1)S(1)}, u32[]{:S(2)}, u32[]{:S(2)}) %all-to-all-start) | async-done | bytes 229408 | tf_op jit(solution)/shard_map/all_to_all | solution.py:36
  32.3 1.8 %fusion.50 = f32[16,128]{1,0:T(8,128)S(1)} fusion(bf16[16,7168]{1,0:T(8,128)(2,1)S(1)} %reshape.465, bf16[7168,128]{1,0:T(8,128)(2,1)} %param.17), kind=kOutput, calls=%fused_computation.71 | convolution fusion | flops 29360128 | bytes 2072576 | tf_op jit(solution)/shard_map/dot_general | solution.py:41
  34.1 2.2 %convolution_convert_fusion.2 = bf16[16,7168]{1,0:T(8,128)(2,1)S(1)} fusion(bf16[128,7168]{1,0:T(8,128)(2,1)} %param.19, bf16[16,7168]{1,0:T(8,128)(2,1)S(1)} %reshape.465, bf16[7168,128]{1,0:T(8,128)(2,1)S(1)} %copy-done, f32[16,128]{1,0:T(8,128)S(1)} %fusion.50), kind=kOutput, calls=%fused_computation.4 | convolution fusion | flops 58847232 | bytes 4136960 | tf_op jit(solution)/shard_map/dot_general | solution.py:44
  36.3 0.8 %reshape.466 = bf16[8,2,7168]{2,1,0:T(2,128)(2,1)} reshape(bf16[16,7168]{1,0:T(8,128)(2,1)S(1)} %convolution_convert_fusion.2) | data formatting | bytes 458752 | tf_op jit(solution)/shard_map/reshape | solution.py:45
  37.1 3.4 %all-to-all-start.1 = ((bf16[8,2,7168]{2,1,0:T(2,128)(2,1)}), bf16[8,2,7168]{2,1,0:T(2,128)(2,1)S(1)}, u32[]{:S(2)}, u32[]{:S(2)}) async-start(bf16[8,2,7168]{2,1,0:T(2,128)(2,1)} %reshape.466), calls=%async_computation.1 | async-start | bytes 458752 | tf_op jit(solution)/shard_map/all_to_all | solution.py:68
  40.5 2.1 %fusion.22 = f32[16,7168]{1,0:T(8,128)S(1)} fusion(bf16[7168,128]{1,0:T(8,128)(2,1)} %param.17, f32[16,128]{1,0:T(8,128)S(1)} %bitcast.48, f32[16,128]{1,0:T(8,128)S(1)} %fusion.51, f32[16,128]{1,0:T(8,128)S(1)} %bitcast.50), kind=kOutput, calls=%fused_computation.37 | convolution fusion | flops 29380608 | bytes 2318336 | tf_op jit(solution)/shard_map/dot_general | solution.py:59
  42.6 0.6 fusion
  43.2 0.8 %reshape.471 = bf16[8,2,7168]{2,1,0:T(2,128)(2,1)} reshape(bf16[16,7168]{1,0:T(8,128)(2,1)S(1)} %fusion) | data formatting | bytes 458752 | tf_op jit(solution)/shard_map/reshape | solution.py:63
  44.0 4.5 %all-to-all-done.1 = bf16[8,2,7168]{2,1,0:T(2,128)(2,1)S(1)} async-done(((bf16[8,2,7168]{2,1,0:T(2,128)(2,1)}), bf16[8,2,7168]{2,1,0:T(2,128)(2,1)S(1)}, u32[]{:S(2)}, u32[]{:S(2)}) %all-to-all-start.1) | async-done | bytes 229408 | tf_op jit(solution)/shard_map/all_to_all | solution.py:68
  48.5 3.4 %all-to-all-start.3 = ((bf16[8,2,7168]{2,1,0:T(2,128)(2,1)}), bf16[8,2,7168]{2,1,0:T(2,128)(2,1)S(1)}, u32[]{:S(2)}, u32[]{:S(2)}) async-start(bf16[8,2,7168]{2,1,0:T(2,128)(2,1)} %reshape.471), calls=%async_computation.3 | async-start | bytes 458752 | tf_op jit(solution)/shard_map/all_to_all | solution.py:68
  51.9 0.2 convert_reduce_fusion.1
  52.1 1.6 %convolution_convert_fusion.1 = bf16[64,7168]{1,0:T(8,128)(2,1)S(1)} fusion(f32[2,7168]{1,0:T(2,128)S(1)} %convert_reduce_fusion.1, f32[64]{0:T(128)S(1)} %get-tuple-element.5, f32[64]{0:T(128)S(1)} %get-tuple-element.6, f32[64]{0:T(128)S(1)} %sub.21), kind=kOutput, calls=%fused_computation.1 | convolution fusion | flops 11469184 | bytes 975616 | tf_op jit(solution)/shard_map/tgc,gcd->td/dot_general | solution.py:70
  53.8 6.1 %all-to-all-done.3 = bf16[8,2,7168]{2,1,0:T(2,128)(2,1)S(1)} async-done(((bf16[8,2,7168]{2,1,0:T(2,128)(2,1)}), bf16[8,2,7168]{2,1,0:T(2,128)(2,1)S(1)}, u32[]{:S(2)}, u32[]{:S(2)}) %all-to-all-start.3) | async-done | bytes 229408 | tf_op jit(solution)/shard_map/all_to_all | solution.py:68
  59.9 0.2 convert_reduce_fusion
  60.1 1.6 %convolution_convert_fusion = bf16[64,7168]{1,0:T(8,128)(2,1)S(1)} fusion(f32[2,7168]{1,0:T(2,128)S(1)} %convert_reduce_fusion, f32[64]{0:T(128)S(1)} %get-tuple-element.7, f32[64]{0:T(128)S(1)} %get-tuple-element.8, f32[64]{0:T(128)S(1)} %sub.22), kind=kOutput, calls=%fused_computation | convolution fusion | flops 11469184 | bytes 975616 | tf_op jit(solution)/shard_map/tgc,gcd->td/dot_general | solution.py:70
  61.8 6.6 %collective-permute-done = bf16[64,7168]{1,0:T(8,128)(2,1)} collective-permute-done((bf16[64,7168]{1,0:T(8,128)(2,1)S(1)}, bf16[64,7168]{1,0:T(8,128)(2,1)}, u32[]{:S(2)}, u32[]{:S(2)}) %collective-permute-start) | collective-permute-done | bytes 917536 | tf_op jit(solution)/shard_map/ppermute | solution.py:13
  68.4 7.0 %collective-permute-done.1 = bf16[64,7168]{1,0:T(8,128)(2,1)S(1)} collective-permute-done((bf16[64,7168]{1,0:T(8,128)(2,1)S(1)}, bf16[64,7168]{1,0:T(8,128)(2,1)S(1)}, u32[]{:S(2)}, u32[]{:S(2)}) %collective-permute-start.1) | collective-permute-done | bytes 917536 | tf_op jit(solution)/shard_map/ppermute | solution.py:13
  75.5 2.3 %fusion.2 = bf16[1,64,7168]{2,1,0:T(8,128)(2,1)} fusion(bf16[64,7168]{1,0:T(8,128)(2,1)S(1)} %collective-permute-done.1, bf16[64,7168]{1,0:T(8,128)(2,1)} %collective-permute-done), kind=kLoop, calls=%fused_computation.10 | loop fusion | flops 1835008 | bytes 2752512 | tf_op jit(solution)/shard_map/broadcast_in_dim | solution.py:89
  (17 shorter events, 0.7 us)
Async XLA Ops:
  0.0 34.1 %copy-start = (bf16[7168,128]{1,0:T(8,128)(2,1)S(1)}, bf16[7168,128]{1,0:T(8,128)(2,1)}, u32[]{:S(2)}) copy-start(bf16[7168,128]{1,0:T(8,128)(2,1)} %param.18) | copy-start | bytes 5505028
  0.0 13.2 %copy-start.1 = (bf16[1,64,7168]{2,1,0:T(8,128)(2,1)S(1)}, bf16[1,64,7168]{2,1,0:T(8,128)(2,1)}, u32[]{:S(2)}) copy-start(bf16[1,64,7168]{2,1,0:T(8,128)(2,1)} %param.10) | copy-start | bytes 2752516
  0.0 24.1 %copy-start.2 = (f32[1,8,2,2,128]{4,3,2,1,0:T(2,128)S(1)}, f32[1,8,2,2,128]{4,3,2,1,0:T(2,128)}, u32[]{:S(2)}) copy-start(f32[1,8,2,2,128]{4,3,2,1,0:T(2,128)} %param.16) | copy-start | bytes 49156
  4.1 15.7 %all-to-all-start.2 = ((bf16[8,2,7168]{2,1,0:T(2,128)(2,1)}), bf16[8,2,7168]{2,1,0:T(2,128)(2,1)S(1)}, u32[]{:S(2)}, u32[]{:S(2)}) async-start(bf16[8,2,7168]{2,1,0:T(2,128)(2,1)} %reshape.469), calls=%async_computation.2 | async-start | bytes 458752 | tf_op jit(solution)/shard_map/all_to_all | solution.py:36
  20.7 11.5 %all-to-all-start = ((bf16[8,2,7168]{2,1,0:T(2,128)(2,1)}), bf16[8,2,7168]{2,1,0:T(2,128)(2,1)S(1)}, u32[]{:S(2)}, u32[]{:S(2)}) async-start(bf16[8,2,7168]{2,1,0:T(2,128)(2,1)} %reshape.464), calls=%async_computation | async-start | bytes 458752 | tf_op jit(solution)/shard_map/all_to_all | solution.py:36
  37.1 11.4 %all-to-all-start.1 = ((bf16[8,2,7168]{2,1,0:T(2,128)(2,1)}), bf16[8,2,7168]{2,1,0:T(2,128)(2,1)S(1)}, u32[]{:S(2)}, u32[]{:S(2)}) async-start(bf16[8,2,7168]{2,1,0:T(2,128)(2,1)} %reshape.466), calls=%async_computation.1 | async-start | bytes 458752 | tf_op jit(solution)/shard_map/all_to_all | solution.py:68
  48.5 11.4 %all-to-all-start.3 = ((bf16[8,2,7168]{2,1,0:T(2,128)(2,1)}), bf16[8,2,7168]{2,1,0:T(2,128)(2,1)S(1)}, u32[]{:S(2)}, u32[]{:S(2)}) async-start(bf16[8,2,7168]{2,1,0:T(2,128)(2,1)} %reshape.471), calls=%async_computation.3 | async-start | bytes 458752 | tf_op jit(solution)/shard_map/all_to_all | solution.py:68
  53.7 14.7 %collective-permute-start = (bf16[64,7168]{1,0:T(8,128)(2,1)S(1)}, bf16[64,7168]{1,0:T(8,128)(2,1)}, u32[]{:S(2)}, u32[]{:S(2)}) collective-permute-start(bf16[64,7168]{1,0:T(8,128)(2,1)S(1)} %convolution_convert_fusion.1), channel_id=1, source_target_pairs={{0,8},{8,16},{16,24},{24,0},{1,9},{9,17},{17,25},{25,1},{2,10},{10... | collective-permute-start | bytes 2752520 | tf_op jit(solution)/shard_map/ppermute | solution.py:13
  61.7 13.7 %collective-permute-start.1 = (bf16[64,7168]{1,0:T(8,128)(2,1)S(1)}, bf16[64,7168]{1,0:T(8,128)(2,1)S(1)}, u32[]{:S(2)}, u32[]{:S(2)}) collective-permute-start(bf16[64,7168]{1,0:T(8,128)(2,1)S(1)} %convolution_convert_fusion), channel_id=1, source_target_pairs={{0,24},{8,0},{16,8},{24,16},{1,25},{9,1},{17,9},{25,17},{2,26},{10... | collective-permute-start | bytes 2752520 | tf_op jit(solution)/shard_map/ppermute | solution.py:13
where the time goes:
time: 78.9 us; the launch traced here: 77.8 us
  waiting for transfers between devices  36.6 us (46%)
  starting transfers between devices  17.6 us (22%)
  matrix products  13.7 us (17%)
  other arithmetic  6.12 us (8%)
  local copies, waits for them, and re-layouts  3.59 us (5%)
    ppermute x2, waiting for transfers between devices, shifted(): return lax.ppermute(value, axis, pairs)  13.7 us
    all_to_all x2, waiting for transfers between devices, dispatch(): lax.all_to_all(outgoing, 'ep', split_axis=0, concat_axis=0, tiled=True)  12.3 us
    all_to_all x2, starting transfers between devices, dispatch(): lax.all_to_all(outgoing, 'ep', split_axis=0, concat_axis=0, tiled=True)  10.7 us
    all_to_all x2, waiting for transfers between devices, combine(): lax.all_to_all(partial_value, 'ep', split_axis=0, concat_axis=0, tiled=True)  10.6 us
    all_to_all x2, starting transfers between devices, combine(): lax.all_to_all(partial_value, 'ep', split_axis=0, concat_axis=0, tiled=True)  6.8 us
    dot_general x2, matrix products, combine(): jnp.einsum('tgc,gcd->td', weighted, summed, precision=lax.Precision.HIGHEST)  3.28 us
    broadcast_in_dim x1, other arithmetic, body(): return total.astype(jnp.bfloat16)[None]  2.31 us
    dot_general x1, matrix products, forward_partial(): jnp.dot(hidden, w_down, preferred_element_type=jnp.float32)  2.18 us
  transfers between devices with their start and end apart: 6, of which 6 were waited for; matrix products, arithmetic and copies ran while one was open for 14% of the time, Pallas kernels for 0%

commit v1 on v0

v1 whole, which is shorter than its diff:
```python
import functools

import jax
import jax.numpy as jnp
from jax import lax
from jax.experimental import pallas as pl
from jax.experimental.pallas import tpu as pltpu
from jax.sharding import PartitionSpec as P

SPLIT = 8
CAP = 2
SUB = 8
PAIR = 2
MESH = pl.DeviceIdType.MESH
BF = jnp.bfloat16
F32 = jnp.float32
NT = (((1,), (1,)), ((), ()))
TN = (((0,), (0,)), ((), ()))


def each(count, step):
    if count <= 4:
        for at in range(count):
            step(at)
    else:
        lax.fori_loop(0, count, lambda at, carry: (step(at), carry)[1], 0)


def route_tables(routes, scores, groups):
    tokens, topk = routes.shape
    weight = 2.5 * scores / jnp.sum(scores, axis=-1, keepdims=True)
    earlier = lax.broadcasted_iota(jnp.int32, (tokens, tokens), 0)
    later = lax.broadcasted_iota(jnp.int32, (tokens, tokens), 1)
    order = (earlier < later).astype(F32)
    ones = jnp.ones((CAP * SUB, topk), F32)
    slot = lax.broadcasted_iota(jnp.int32, (CAP * SUB, tokens), 0) // SUB
    placed, weighted = [], []
    for group in range(groups):
        match = (routes == group).astype(F32)
        hits = lax.dot_general(ones, match, NT, preferred_element_type=F32)
        shares = lax.dot_general(
            ones, match * weight, NT, precision=lax.Precision.HIGHEST, preferred_element_type=F32
        )
        before = jnp.dot(hits, order, preferred_element_type=F32)
        here = hits * (before == slot.astype(F32)).astype(F32)
        placed.append(here)
        weighted.append(here * shares)
    return placed, weighted


def sub_mask(rows, lanes, part):
    return lax.broadcasted_iota(jnp.int32, (rows, lanes), 0) % SUB == part


def kernel(
    axes, groups,
    x_hbm, dy_hbm, rf_hbm, rb_hbm, sf_hbm, sb_hbm, saved_hbm, wg_hbm, wu_hbm, wd_hbm,
    total_ref, table_ref,
    x_s, dy_s, route_s, score_s, saved_s, wgu_s, wd_s,
    slots, rows, hid, grad, away, mine, pair_in, pair_out, final_in, table_s,
    load_sem, z_send, z_recv, y_send, y_recv, a_send, a_recv, f_send, f_recv, t_send, t_recv,
):
    sections, ep = axes
    high = ep // PAIR
    per_group = SPLIT // PAIR
    width = slots.shape[-1]
    hidden = wd_s.shape[1]
    p = lax.axis_index("pp")
    e = lax.axis_index("ep")
    hi, lo = e // PAIR, lax.rem(e, PAIR)
    other = 1 - lo
    after, before = lax.rem(p + 1, sections), lax.rem(p + sections - 1, sections)
    ahead = (after, before)

    loads = [
        pltpu.make_async_copy(rf_hbm, route_s.at[0], load_sem.at[0]),
        pltpu.make_async_copy(rb_hbm, route_s.at[1], load_sem.at[1]),
        pltpu.make_async_copy(sf_hbm, score_s.at[0], load_sem.at[2]),
        pltpu.make_async_copy(sb_hbm, score_s.at[1], load_sem.at[3]),
        pltpu.make_async_copy(x_hbm, x_s, load_sem.at[4]),
        pltpu.make_async_copy(dy_hbm, dy_s, load_sem.at[5]),
        pltpu.make_async_copy(saved_hbm, saved_s, load_sem.at[6]),
        pltpu.make_async_copy(wg_hbm, wgu_s.at[:, pl.ds(0, hidden)], load_sem.at[7]),
        pltpu.make_async_copy(wu_hbm, wgu_s.at[:, pl.ds(hidden, hidden)], load_sem.at[8]),
    ] + [
        pltpu.make_async_copy(wd_hbm.at[:, pl.ds(part * width, width)], wd_s.at[part], load_sem.at[9 + part])
        for part in range(SUB)
    ]
    for load in loads:
        load.start()

    barrier = pltpu.get_barrier_semaphore()

    def greet(section, at):
        pl.semaphore_signal(barrier, inc=1, device_id=(section, at), device_id_type=MESH)

    greet(p, hi * PAIR + other)
    each(high - 1, lambda k: greet(p, lax.rem(hi + k + 1, high) * PAIR + lo))
    each(high, lambda k: greet(after, lax.rem(hi + k, high) * PAIR + lo))
    each(high, lambda k: greet(before, lax.rem(hi + k, high) * PAIR + lo))

    for load in loads[:4]:
        load.wait()
    tables = [route_tables(route_s[d], score_s[d], groups) for d in range(2)]
    for d in range(2):
        for group in range(groups):
            table_s[d, pl.ds(group * CAP * SUB, CAP * SUB), :] = tables[d][1][group]

    def z_copy(d, k):
        to = lax.rem(hi + k, high)
        return pltpu.make_async_remote_copy(
            slots.at[d, to // per_group], rows.at[d, hi, lo],
            z_send.at[d, k], z_recv.at[d, k], (p, to * PAIR + lo), MESH,
        )

    def y_copy(d, k):
        block = lax.rem(hi + high - k, high)
        return pltpu.make_async_remote_copy(
            rows.at[d, block, lo], rows.at[d, block, lo],
            y_send.at[d, k], y_recv.at[d, k], (p, hi * PAIR + other), MESH,
        )

    def t_copy(d):
        return pltpu.make_async_remote_copy(
            table_s.at[d], table_ref.at[d], t_send.at[d], t_recv.at[d], (ahead[d], e), MESH
        )

    def pick(d):
        tokens = (x_s, dy_s)[d]
        loads[4 + d].wait()
        for group in range(groups):
            acc = jnp.zeros((CAP * SUB, width), F32)
            placed = tables[d][0][group]
            for part in range(SUB):
                chosen = jnp.where(sub_mask(CAP * SUB, placed.shape[1], part), placed, 0.0).astype(BF)
                acc += jnp.dot(
                    chosen, tokens[:, part * width:(part + 1) * width], preferred_element_type=F32
                )
            slots[d, group] = acc.astype(BF)
        rows[d, hi, lo] = slots[d, hi // per_group]

    pick(0)
    pl.semaphore_wait(barrier, PAIR - 1 + 3 * high - 1)
    for d in range(2):
        if d:
            pick(d)
        each(high - 1, lambda k, d=d: z_copy(d, k + 1).start())
        y_copy(d, 0).start()
    for d in range(2):
        t_copy(d).start()

    def relay(d):
        def step(k):
            z_copy(d, k + 1).wait_recv()
            y_copy(d, k + 1).start()
        each(high - 1, step)

    def gathered(d):
        each(high, lambda k: y_copy_in(d, k).wait_recv())

    def y_copy_in(d, k):
        block = lax.rem(hi + high - k, high)
        return pltpu.make_async_remote_copy(
            rows.at[d, block, other], rows.at[d, block, other],
            y_send.at[d, k], y_recv.at[d, k], (p, hi * PAIR + other), MESH,
        )

    relay(0)
    relay(1)

    block_rows = CAP * SUB
    step_high = min(high, 4)
    chunks = high // step_high
    full = step_high * PAIR * block_rows
    half = step_high * block_rows

    def spread(value):
        count, lanes = value.shape
        summed = jnp.sum(value.reshape(count // SUB, SUB, lanes), axis=1, keepdims=True)
        return jnp.broadcast_to(summed, (count // SUB, SUB, lanes)).reshape(count, lanes)

    def at_chunk(chunk):
        return pl.ds(chunk * step_high, step_high)

    def forward_hidden(chunk):
        held = rows[0, at_chunk(chunk)].reshape(full, width)
        acc = jnp.zeros((full, 2 * hidden), F32)
        for part in range(SUB):
            acc += jnp.dot(
                jnp.where(sub_mask(full, width, part), held, jnp.zeros_like(held)),
                wgu_s[pl.ds(part * width, width), :], preferred_element_type=F32,
            )
        pre = spread(acc)
        gate, up = pre[:, :hidden], pre[:, hidden:]
        value = (gate / (1.0 + jnp.exp(-gate)) * up).astype(BF)
        hid[at_chunk(chunk)] = value.reshape(step_high, PAIR, block_rows, hidden)

    def backward_hidden(chunk):
        held = rows[1, at_chunk(chunk)].reshape(full, width)
        acc = jnp.zeros((full, hidden), F32)
        for part in range(SUB):
            acc += lax.dot_general(
                jnp.where(sub_mask(full, width, part), held, jnp.zeros_like(held)),
                wd_s[part], NT, preferred_element_type=F32,
            )
        grad_hidden = spread(acc)
        count = step_high * PAIR * CAP
        kept = saved_s[pl.ds(chunk * count, count)]
        gate = jnp.broadcast_to(kept[:, 0:1, :], (count, SUB, hidden)).reshape(full, hidden)
        up = jnp.broadcast_to(kept[:, 1:2, :], (count, SUB, hidden)).reshape(full, hidden)
        sigma = 1.0 / (1.0 + jnp.exp(-gate))
        grad_gate = (grad_hidden * up * sigma * (1.0 + gate * (1.0 - sigma))).astype(BF)
        grad_up = (grad_hidden * gate * sigma).astype(BF)
        both = jnp.concatenate([grad_gate, grad_up], axis=1)
        grad[at_chunk(chunk)] = both.reshape(step_high, PAIR, block_rows, 2 * hidden)

    def forward_out(chunk, side):
        held = hid[at_chunk(chunk), side].reshape(half, hidden)
        parts = [
            jnp.where(sub_mask(half, hidden, part), held, jnp.zeros_like(held)) for part in range(SUB)
        ]
        return jnp.dot(
            jnp.concatenate(parts, axis=1), wd_s[...].reshape(SUB * hidden, width),
            preferred_element_type=F32,
        )

    def backward_out(chunk, side):
        held = grad[at_chunk(chunk), side].reshape(half, 2 * hidden)
        acc = jnp.zeros((half, width), F32)
        for part in range(SUB):
            acc += lax.dot_general(
                jnp.where(sub_mask(half, 2 * hidden, part), held, jnp.zeros_like(held)),
                wgu_s[pl.ds(part * width, width), :], NT, preferred_element_type=F32,
            )
        return acc

    outs = (forward_out, backward_out)

    def a_copy(d, k):
        block = lax.rem(hi + k, high)
        return pltpu.make_async_remote_copy(
            away.at[d, block], pair_in.at[d, block],
            a_send.at[d, k], a_recv.at[d, k], (p, hi * PAIR + other), MESH,
        )

    def f_copy(d, k):
        block = lax.rem(hi + k, high)
        return pltpu.make_async_remote_copy(
            pair_out.at[d, block], final_in.at[d, hi],
            f_send.at[d, k], f_recv.at[d, k], (ahead[d], block * PAIR + lo), MESH,
        )

    def f_copy_in(d, k):
        block = lax.rem(hi + high - k, high)
        return pltpu.make_async_remote_copy(
            pair_out.at[d, block], final_in.at[d, block],
            f_send.at[d, k], f_recv.at[d, k], (ahead[d], block * PAIR + lo), MESH,
        )

    def partial(d):
        def out_away(chunk):
            away[d, at_chunk(chunk)] = outs[d](chunk, other).astype(BF).reshape(step_high, block_rows, width)
        each(chunks, out_away)
        each(high, lambda k: a_copy(d, k).start())

        def out_mine(chunk):
            mine[d, at_chunk(chunk)] = outs[d](chunk, lo).reshape(step_high, block_rows, width)
        each(chunks, out_mine)

    def pass_on(d):
        def step(k):
            block = lax.rem(hi + k, high)
            a_copy(d, k).wait_recv()
            pair_out[d, block] = (mine[d, block] + pair_in[d, block].astype(F32)).astype(BF)
            f_copy(d, k).start()
        each(high, step)

    for load in loads[6:]:
        load.wait()
    gathered(0)
    each(chunks, forward_hidden)
    partial(0)
    gathered(1)
    each(chunks, backward_hidden)
    pass_on(0)
    partial(1)
    pass_on(1)

    for d in range(2):
        each(high, lambda k, d=d: f_copy_in(d, k).wait_recv())
        for group in range(groups):
            acc = final_in[d, group * per_group].astype(F32)
            for at in range(1, per_group):
                acc += final_in[d, group * per_group + at].astype(F32)
            total_ref[d, pl.ds(group * block_rows, block_rows), :] = acc
        t_copy(d).wait_recv()

    for d in range(2):
        t_copy(d).wait_send()
        each(high - 1, lambda k, d=d: z_copy(d, k + 1).wait_send())
        each(high, lambda k, d=d: y_copy(d, k).wait_send())
        each(high, lambda k, d=d: a_copy(d, k).wait_send())
        each(high, lambda k, d=d: f_copy(d, k).wait_send())


def combine_kernel(groups, total_ref, table_ref, out_ref, column_s):
    part = pl.program_id(0)
    count = table_ref.shape[1]

    @pl.when(part == 0)
    def _():
        row = lax.broadcasted_iota(jnp.int32, (count, count), 0)
        col = lax.broadcasted_iota(jnp.int32, (count, count), 1)
        same = (row == col).astype(F32)
        for d in range(2):
            column_s[d] = lax.dot_general(
                table_ref[d], same, TN, precision=lax.Precision.HIGHEST, preferred_element_type=F32
            )

    routed = []
    for d in range(2):
        acc = None
        for slot in range(groups * CAP):
            term = column_s[d, :, slot * SUB:slot * SUB + 1] * total_ref[d, pl.ds(slot * SUB + part, 1), :]
            acc = term if acc is None else acc + term
        routed.append(acc.astype(BF).astype(F32))
    out_ref[0] = (routed[0] + routed[1]).astype(BF)


def solution(mesh):
    sections, ep = mesh.shape["pp"], mesh.shape["ep"]
    groups = ep // SPLIT
    high = ep // PAIR

    def body(x, dy, rf, rb, sf, sb, saved, wg, wu, wd):
        _, tokens, model = x.shape
        topk = rf.shape[2]
        hidden = wg.shape[1]
        width = model // SUB
        block_rows = CAP * SUB
        anywhere = pl.BlockSpec(memory_space=pl.ANY)
        vmem = pl.BlockSpec(memory_space=pltpu.VMEM)
        total, table = pl.pallas_call(
            functools.partial(kernel, (sections, ep), groups),
            out_shape=(
                jax.ShapeDtypeStruct((2, groups * block_rows, width), F32),
                jax.ShapeDtypeStruct((2, groups * block_rows, tokens), F32),
            ),
            in_specs=[anywhere] * 10,
            out_specs=(vmem, vmem),
            scratch_shapes=[
                pltpu.VMEM((tokens, model), BF),
                pltpu.VMEM((tokens, model), BF),
                pltpu.VMEM((2, tokens, topk), jnp.int32),
                pltpu.VMEM((2, tokens, topk), F32),
                pltpu.VMEM((ep * CAP, 2, hidden), F32),
                pltpu.VMEM((model, 2 * hidden), BF),
                pltpu.VMEM((SUB, hidden, width), BF),
                pltpu.VMEM((2, groups, block_rows, width), BF),
                pltpu.VMEM((2, high, PAIR, block_rows, width), BF),
                pltpu.VMEM((high, PAIR, block_rows, hidden), BF),
                pltpu.VMEM((high, PAIR, block_rows, 2 * hidden), BF),
                pltpu.VMEM((2, high, block_rows, width), BF),
                pltpu.VMEM((2, high, block_rows, width), F32),
                pltpu.VMEM((2, high, block_rows, width), BF),
                pltpu.VMEM((2, high, block_rows, width), BF),
                pltpu.VMEM((2, high, block_rows, width), BF),
                pltpu.VMEM((2, groups * block_rows, tokens), F32),
                pltpu.SemaphoreType.DMA((9 + SUB,)),
            ] + [pltpu.SemaphoreType.DMA((2, high))] * 8 + [pltpu.SemaphoreType.DMA((2,))] * 2,
            compiler_params=pltpu.CompilerParams(
                collective_id=0, has_side_effects=True, vmem_limit_bytes=48 * 1024 * 1024
            ),
            name="experts",
        )(x[0], dy[0], rf[0], rb[0], sf[0], sb[0], saved.reshape(ep * CAP, 2, hidden), wg, wu, wd)
        return pl.pallas_call(
            functools.partial(combine_kernel, groups),
            grid=(SUB,),
            out_shape=jax.ShapeDtypeStruct((1, tokens, model), BF),
            in_specs=[
                pl.BlockSpec(total.shape, lambda part: (0, 0, 0)),
                pl.BlockSpec(table.shape, lambda part: (0, 0, 0)),
            ],
            out_specs=pl.BlockSpec((1, tokens, width), lambda part: (0, 0, part)),
            scratch_shapes=[pltpu.VMEM((2, tokens, groups * block_rows), F32)],
            name="combine",
        )(total, table)

    in_specs = (
        P("pp", "ep", None),
        P("pp", "ep", None),
        P("pp", "ep", None),
        P("pp", "ep", None),
        P("pp", "ep", None),
        P("pp", "ep", None),
        P("pp", None, None, None, "ep"),
        P(None, "ep"),
        P(None, "ep"),
        P("ep", None),
    )
    out_specs = P("pp", "ep", None)
    return jax.shard_map(body, mesh=mesh, in_specs=in_specs, out_specs=out_specs, check_vma=False)
```

time: 78.9 us -> 46 us (0.58)
  the two profiles are of different devices: /device:TPU:0 before, /device:TPU:1 now
where the time goes in v1:
time: 46 us; the launch traced here: 45.6 us
  Pallas kernels  35.2 us (77%)
  local copies, waits for them, and re-layouts  10.4 us (23%)
    pallas_call x1, Pallas kernels, body(): pl.pallas_call(functools.partial(kernel, (sections, ep), groups), out_sha...  30.7 us
    unnamed x18, local copies, waits for them, and re-layouts  10.4 us
    pallas_call x1, Pallas kernels, body(): pl.pallas_call(functools.partial(combine_kernel, groups), grid=(SUB,), ou...  4.52 us

profile of v1, /device:TPU:1, one launch (start us, length us, event | category | flops | bytes accessed | tf_op | source)
XLA Modules:
  0.0 45.6 jit_solution(4567029752206583059)
XLA Ops:
  0.0 0.8 %copy.11 = s32[1,64,8]{2,1,0:T(8,128)S(1)} copy(s32[1,64,8]{1,2,0:T(8,128)} %param.12) | data formatting | bytes 4096 | tf_op args[2]
  0.8 0.8 %copy.12 = s32[1,64,8]{2,1,0:T(8,128)S(1)} copy(s32[1,64,8]{1,2,0:T(8,128)} %param.13) | data formatting | bytes 4096 | tf_op args[3]
  1.5 0.8 %copy.13 = f32[1,64,8]{2,1,0:T(8,128)S(1)} copy(f32[1,64,8]{1,2,0:T(8,128)} %param.14) | data formatting | bytes 4096 | tf_op args[4]
  2.3 0.8 %copy.14 = f32[1,64,8]{2,1,0:T(8,128)S(1)} copy(f32[1,64,8]{1,2,0:T(8,128)} %param.15) | data formatting | bytes 4096 | tf_op args[5]
  3.1 0.0 copy-start
  3.1 1.5 %copy-done = bf16[7168,128]{1,0:T(8,128)(2,1)S(1)} copy-done((bf16[7168,128]{1,0:T(8,128)(2,1)S(1)}, bf16[7168,128]{1,0:T(8,128)(2,1)}, u32[]{:S(2)}) %copy-start) | copy-done | bytes 1835032
  4.6 0.0 copy-start.1
  4.6 1.5 %copy-done.1 = bf16[7168,128]{1,0:T(8,128)(2,1)S(1)} copy-done((bf16[7168,128]{1,0:T(8,128)(2,1)S(1)}, bf16[7168,128]{1,0:T(8,128)(2,1)}, u32[]{:S(2)}) %copy-start.1) | copy-done | bytes 1835032
  6.1 0.0 copy-start.2
  6.1 1.2 %copy-done.2 = bf16[1,64,7168]{2,1,0:T(8,128)(2,1)S(1)} copy-done((bf16[1,64,7168]{2,1,0:T(8,128)(2,1)S(1)}, bf16[1,64,7168]{2,1,0:T(8,128)(2,1)}, u32[]{:S(2)}) %copy-start.2) | copy-done | bytes 917528
  7.3 0.0 copy-start.3
  7.3 1.2 %copy-done.3 = bf16[1,64,7168]{2,1,0:T(8,128)(2,1)S(1)} copy-done((bf16[1,64,7168]{2,1,0:T(8,128)(2,1)S(1)}, bf16[1,64,7168]{2,1,0:T(8,128)(2,1)}, u32[]{:S(2)}) %copy-start.3) | copy-done | bytes 917528
  8.4 0.0 copy-start.5
  8.4 0.7 %copy-done.5 = f32[1,8,2,2,128]{4,3,2,1,0:T(2,128)S(1)} copy-done((f32[1,8,2,2,128]{4,3,2,1,0:T(2,128)S(1)}, f32[1,8,2,2,128]{4,3,2,1,0:T(2,128)}, u32[]{:S(2)}) %copy-start.5) | copy-done | bytes 16408
  9.2 30.7 %experts.1 = (f32[2,16,896]{2,1,0:T(8,128)S(1)}, f32[2,16,64]{2,1,0:T(8,128)S(1)}) custom-call(bf16[64,7168]{1,0:T(8,128)(2,1)S(1)} %bitcast.7, bf16[64,7168]{1,0:T(8,128)(2,1)S(1)} %bitcast.8, s32[64,8]{1,0:T(8,128)S(1)} %bitcast.9, s32[64,8]{1,0:T(8,128)S(1)} %bitcast.10, f32[64,8]{1,0:T(8,128)S(1)} %bitcast.11, f32[64,8]{1,0:T(8,128)S(1)} %bitcast.12, ...), custom_call_target="tpu_custom_call" | custom-call | tf_op jit(solution)/shard_map/experts/pallas_call | solution.py:343
  39.8 0.0 copy-start.4
  39.8 0.6 %copy-done.4 = f32[2,16,896]{2,1,0:T(8,128)} copy-done((f32[2,16,896]{2,1,0:T(8,128)}, f32[2,16,896]{2,1,0:T(8,128)S(1)}, u32[]{:S(2)}) %copy-start.4) | copy-done | bytes 114712
  40.5 0.0 copy-start.6
  40.5 0.6 %copy-done.6 = f32[2,16,64]{2,1,0:T(8,128)} copy-done((f32[2,16,64]{2,1,0:T(8,128)}, f32[2,16,64]{2,1,0:T(8,128)S(1)}, u32[]{:S(2)}) %copy-start.6) | copy-done | bytes 8216
  41.1 4.5 %combine.1 = bf16[1,64,7168]{2,1,0:T(8,128)(2,1)} custom-call(f32[2,16,896]{2,1,0:T(8,128)} %copy-done.4, f32[2,16,64]{2,1,0:T(8,128)} %copy-done.6), custom_call_target="tpu_custom_call" | custom-call | tf_op jit(solution)/shard_map/combine/pallas_call | solution.py:376
Async XLA Ops:
  3.1 1.5 %copy-start = (bf16[7168,128]{1,0:T(8,128)(2,1)S(1)}, bf16[7168,128]{1,0:T(8,128)(2,1)}, u32[]{:S(2)}) copy-start(bf16[7168,128]{1,0:T(8,128)(2,1)} %wg_hbm.1) | copy-start | bytes 5505028
  4.6 1.5 %copy-start.1 = (bf16[7168,128]{1,0:T(8,128)(2,1)S(1)}, bf16[7168,128]{1,0:T(8,128)(2,1)}, u32[]{:S(2)}) copy-start(bf16[7168,128]{1,0:T(8,128)(2,1)} %wu_hbm.1) | copy-start | bytes 5505028
  6.1 1.2 %copy-start.2 = (bf16[1,64,7168]{2,1,0:T(8,128)(2,1)S(1)}, bf16[1,64,7168]{2,1,0:T(8,128)(2,1)}, u32[]{:S(2)}) copy-start(bf16[1,64,7168]{2,1,0:T(8,128)(2,1)} %param.10) | copy-start | bytes 2752516
  7.3 1.2 %copy-start.3 = (bf16[1,64,7168]{2,1,0:T(8,128)(2,1)S(1)}, bf16[1,64,7168]{2,1,0:T(8,128)(2,1)}, u32[]{:S(2)}) copy-start(bf16[1,64,7168]{2,1,0:T(8,128)(2,1)} %param.11) | copy-start | bytes 2752516
  8.4 0.7 %copy-start.5 = (f32[1,8,2,2,128]{4,3,2,1,0:T(2,128)S(1)}, f32[1,8,2,2,128]{4,3,2,1,0:T(2,128)}, u32[]{:S(2)}) copy-start(f32[1,8,2,2,128]{4,3,2,1,0:T(2,128)} %param.16) | copy-start | bytes 49156
  39.8 0.6 %copy-start.4 = (f32[2,16,896]{2,1,0:T(8,128)}, f32[2,16,896]{2,1,0:T(8,128)S(1)}, u32[]{:S(2)}) copy-start(f32[2,16,896]{2,1,0:T(8,128)S(1)} %get-tuple-element.7.total_ref) | copy-start | bytes 344068
  40.5 0.6 %copy-start.6 = (f32[2,16,64]{2,1,0:T(8,128)}, f32[2,16,64]{2,1,0:T(8,128)S(1)}, u32[]{:S(2)}) copy-start(f32[2,16,64]{2,1,0:T(8,128)S(1)} %get-tuple-element.8.table_ref) | copy-start | bytes 24580

commit v2 on v1

v2 whole, which is shorter than its diff:
```python
import functools

import jax
import jax.numpy as jnp
from jax import lax
from jax.experimental import pallas as pl
from jax.experimental.pallas import tpu as pltpu
from jax.sharding import PartitionSpec as P

SPLIT = 8
CAP = 2
SUB = 8
PAIR = 2
VMEM_BYTES = 60 * 1024 * 1024
MESH = pl.DeviceIdType.MESH
BF = jnp.bfloat16
F32 = jnp.float32
NT = (((1,), (1,)), ((), ()))
TN = (((0,), (0,)), ((), ()))


def each(count, step):
    if count <= 4:
        for at in range(count):
            step(at)
    else:
        lax.fori_loop(0, count, lambda at, carry: (step(at), carry)[1], 0)


def route_tables(routes, scores, groups):
    tokens = routes.shape[1]
    weight = 2.5 * scores / jnp.sum(scores, axis=0, keepdims=True)
    earlier = lax.broadcasted_iota(jnp.int32, (tokens, tokens), 0)
    later = lax.broadcasted_iota(jnp.int32, (tokens, tokens), 1)
    order = (earlier < later).astype(F32)
    rows = CAP * SUB
    slot = (lax.broadcasted_iota(jnp.int32, (rows, tokens), 0) // SUB).astype(F32)
    placed, weighted = [], []
    for group in range(groups):
        match = (routes == group).astype(F32)
        hits = jnp.broadcast_to(jnp.sum(match, axis=0, keepdims=True), (rows, tokens))
        shares = jnp.broadcast_to(jnp.sum(match * weight, axis=0, keepdims=True), (rows, tokens))
        before = jnp.dot(hits, order, preferred_element_type=F32)
        here = hits * (before == slot).astype(F32)
        placed.append(here)
        weighted.append(here * shares)
    return placed, weighted


def masks(lanes):
    part = lax.broadcasted_iota(jnp.int32, (CAP * SUB, lanes), 0) & (SUB - 1)
    return [part == at for at in range(SUB)]


def masked(held, mask):
    blocks, rows, lanes = held.shape
    return jnp.where(mask[None], held, jnp.zeros_like(held)).reshape(blocks * rows, lanes)


def kernel(
    axes, groups, lane_chunks,
    x_hbm, dy_hbm, rf_hbm, rb_hbm, sf_hbm, sb_hbm, saved_hbm, wg_hbm, wu_hbm, wd_hbm,
    out_hbm,
    tokens_s, route_s, score_s, saved_s, wgu_s, wd_s,
    slots, rows, hid, grad, away, mine, pair_in, pair_out, final_in, table_s, table_in, routed_s, out_s,
    load_sem, out_sem, z_send, z_recv, y_send, y_recv, a_send, a_recv, f_send, f_recv, t_send, t_recv,
):
    sections, ep = axes
    high = ep // PAIR
    per_group = SPLIT // PAIR
    width = slots.shape[-1]
    count = x_hbm.shape[0]
    hidden = wd_s.shape[0] // SUB
    p = lax.axis_index("pp")
    e = lax.axis_index("ep")
    hi, lo = e // PAIR, lax.rem(e, PAIR)
    other = 1 - lo
    after, before = lax.rem(p + 1, sections), lax.rem(p + sections - 1, sections)
    ahead = (after, before)

    def columns(part):
        return pl.ds(part * width, width)

    small = [
        pltpu.make_async_copy(rf_hbm, route_s.at[0], load_sem.at[0]),
        pltpu.make_async_copy(rb_hbm, route_s.at[1], load_sem.at[1]),
        pltpu.make_async_copy(sf_hbm, score_s.at[0], load_sem.at[2]),
        pltpu.make_async_copy(sb_hbm, score_s.at[1], load_sem.at[3]),
    ]
    inputs = [
        [
            pltpu.make_async_copy(
                hbm.at[:, columns(part)], tokens_s.at[d, pl.ds(part * count, count)],
                load_sem.at[4 + d * SUB + part],
            )
            for part in range(SUB)
        ]
        for d, hbm in enumerate((x_hbm, dy_hbm))
    ]
    first = 4 + 2 * SUB
    saved_load = [pltpu.make_async_copy(saved_hbm, saved_s, load_sem.at[first + 3 * SUB])]
    up_loads = [
        pltpu.make_async_copy(
            hbm.at[columns(part), :],
            wgu_s.at[:, pl.ds((2 * part + side) * hidden, hidden)],
            load_sem.at[first + side * SUB + part],
        )
        for part in range(SUB)
        for side, hbm in enumerate((wg_hbm, wu_hbm))
    ]
    down_loads = [
        pltpu.make_async_copy(
            wd_hbm.at[:, columns(part)], wd_s.at[pl.ds(part * hidden, hidden)],
            load_sem.at[first + 2 * SUB + part],
        )
        for part in range(SUB)
    ]
    for load in small + inputs[0]:
        load.start()

    barrier = pltpu.get_barrier_semaphore()

    def greet(section, at):
        pl.semaphore_signal(barrier, inc=1, device_id=(section, at), device_id_type=MESH)

    greet(p, hi * PAIR + other)
    each(high - 1, lambda k: greet(p, lax.rem(hi + k + 1, high) * PAIR + lo))
    each(high, lambda k: greet(after, lax.rem(hi + k, high) * PAIR + lo))
    each(high, lambda k: greet(before, lax.rem(hi + k, high) * PAIR + lo))

    for load in inputs[1] + up_loads + down_loads + saved_load:
        load.start()

    for load in small:
        load.wait()
    tables = [route_tables(route_s[d], score_s[d], groups) for d in range(2)]
    block_rows = CAP * SUB
    for d in range(2):
        for group in range(groups):
            table_s[d, pl.ds(group * block_rows, block_rows), :] = tables[d][1][group]

    def z_copy(d, k):
        to = lax.rem(hi + k, high)
        return pltpu.make_async_remote_copy(
            slots.at[d, to // per_group], rows.at[d, hi, lo],
            z_send.at[d, k], z_recv.at[d, k], (p, to * PAIR + lo), MESH,
        )

    def y_copy(d, k, side):
        block = lax.rem(hi + high - k, high)
        return pltpu.make_async_remote_copy(
            rows.at[d, block, side], rows.at[d, block, side],
            y_send.at[d, k], y_recv.at[d, k], (p, hi * PAIR + other), MESH,
        )

    def t_copy(d):
        return pltpu.make_async_remote_copy(
            table_s.at[d], table_in.at[d], t_send.at[d], t_recv.at[d], (ahead[d], e), MESH
        )

    lanes = SUB * count
    own_part = lax.broadcasted_iota(jnp.int32, (block_rows, lanes), 0) & (SUB - 1)
    same_part = own_part == lax.broadcasted_iota(jnp.int32, (block_rows, lanes), 1) // count

    def pick(d):
        chosen = []
        for group in range(groups):
            wide = jnp.concatenate([tables[d][0][group]] * SUB, axis=1)
            chosen.append(jnp.where(same_part, wide, 0.0).astype(BF))
        for load in inputs[d]:
            load.wait()
        for group in range(groups):
            slots[d, group] = jnp.dot(
                chosen[group], tokens_s[d], preferred_element_type=F32
            ).astype(BF)
        rows[d, hi, lo] = slots[d, hi // per_group]

    pick(0)
    pl.semaphore_wait(barrier, PAIR - 1 + 3 * high - 1)
    for d in range(2):
        if d:
            pick(d)
        each(high - 1, lambda k, d=d: z_copy(d, k + 1).start())
        y_copy(d, 0, lo).start()
    for d in range(2):
        t_copy(d).start()

    def relay(d):
        def step(k):
            z_copy(d, k + 1).wait_recv()
            y_copy(d, k + 1, lo).start()
        each(high - 1, step)

    def gathered(d):
        each(high, lambda k: y_copy(d, k, other).wait_recv())

    step_high = min(high, 4)
    chunks = high // step_high
    blocks = step_high * PAIR
    full = blocks * block_rows
    half = step_high * block_rows

    def spread(value):
        size, wide = value.shape
        summed = jnp.sum(value.reshape(size // SUB, SUB, wide), axis=1, keepdims=True)
        return jnp.broadcast_to(summed, (size // SUB, SUB, wide)).reshape(size, wide)

    def at_chunk(chunk):
        return pl.ds(chunk * step_high, step_high)

    def forward_hidden(chunk):
        held = rows[0, at_chunk(chunk)].reshape(blocks, block_rows, width)
        acc = jnp.zeros((full, 2 * hidden), F32)
        for part, mask in enumerate(masks(width)):
            acc += jnp.dot(
                masked(held, mask), wgu_s[:, pl.ds(part * 2 * hidden, 2 * hidden)],
                preferred_element_type=F32,
            )
        pre = spread(acc)
        gate, up = pre[:, :hidden], pre[:, hidden:]
        value = (gate / (1.0 + jnp.exp(-gate)) * up).astype(BF)
        hid[at_chunk(chunk)] = value.reshape(step_high, PAIR, block_rows, hidden)

    def backward_hidden(chunk):
        held = rows[1, at_chunk(chunk)].reshape(blocks, block_rows, width)
        acc = jnp.zeros((full, hidden), F32)
        for part, mask in enumerate(masks(width)):
            acc += lax.dot_general(
                masked(held, mask), wd_s[pl.ds(part * hidden, hidden), :], NT,
                preferred_element_type=F32,
            )
        grad_hidden = spread(acc)
        size = step_high * PAIR * CAP
        kept = saved_s[pl.ds(chunk * size, size)]
        gate = jnp.broadcast_to(kept[:, 0:1, :], (size, SUB, hidden)).reshape(full, hidden)
        up = jnp.broadcast_to(kept[:, 1:2, :], (size, SUB, hidden)).reshape(full, hidden)
        sigma = 1.0 / (1.0 + jnp.exp(-gate))
        grad_gate = (grad_hidden * up * sigma * (1.0 + gate * (1.0 - sigma))).astype(BF)
        grad_up = (grad_hidden * gate * sigma).astype(BF)
        both = jnp.concatenate([grad_gate, grad_up], axis=1)
        grad[at_chunk(chunk)] = both.reshape(step_high, PAIR, block_rows, 2 * hidden)

    def side_parts(source, chunk):
        held = jnp.concatenate([source[at_chunk(chunk), other], source[at_chunk(chunk), lo]], axis=0)
        return jnp.concatenate([masked(held, mask) for mask in masks(held.shape[-1])], axis=1)

    def forward_out(chunk, cut):
        return jnp.dot(side_parts(hid, chunk), wd_s[:, cut], preferred_element_type=F32)

    def backward_out(chunk, cut):
        return lax.dot_general(side_parts(grad, chunk), wgu_s[cut, :], NT, preferred_element_type=F32)

    outs = (forward_out, backward_out)
    cuts = [pl.ds(low, size) for low, size in lane_chunks]

    def a_copy(d, n):
        return pltpu.make_async_remote_copy(
            away.at[d, :, :, cuts[n]], pair_in.at[d, :, :, cuts[n]],
            a_send.at[d, n], a_recv.at[d, n], (p, hi * PAIR + other), MESH,
        )

    def f_copy(d, n, k, arriving=False):
        block = lax.rem(hi + (high - k if arriving else k), high)
        slot = block if arriving else hi
        return pltpu.make_async_remote_copy(
            pair_out.at[d, block, :, cuts[n]], final_in.at[d, slot, :, cuts[n]],
            f_send.at[d, n, k], f_recv.at[d, n, k], (ahead[d], block * PAIR + lo), MESH,
        )

    def partial(d):
        for n, cut in enumerate(cuts):
            def make(chunk, cut=cut):
                value = outs[d](chunk, cut)
                shape = (step_high, block_rows, value.shape[1])
                away[d, at_chunk(chunk), :, cut] = value[:half].astype(BF).reshape(shape)
                mine[d, at_chunk(chunk), :, cut] = value[half:].reshape(shape)
            each(chunks, make)
            a_copy(d, n).start()

    def pass_on(d):
        for n, cut in enumerate(cuts):
            a_copy(d, n).wait_recv()

            def add(k, n=n, cut=cut):
                block = lax.rem(hi + k, high)
                pair_out[d, block, :, cut] = (
                    mine[d, block, :, cut] + pair_in[d, block, :, cut].astype(F32)
                ).astype(BF)
                f_copy(d, n, k).start()
            each(high, add)

    def route_columns(d):
        t_copy(d).wait_recv()
        size = table_in.shape[1]
        row = lax.broadcasted_iota(jnp.int32, (size, size), 0)
        col = lax.broadcasted_iota(jnp.int32, (size, size), 1)
        return lax.dot_general(
            table_in[d], (row == col).astype(F32), TN,
            precision=lax.Precision.HIGHEST, preferred_element_type=F32,
        )

    def finish(d, table):
        for n in range(len(cuts)):
            each(high, lambda k, n=n: f_copy(d, n, k, True).wait_recv())
        totals = []
        for group in range(groups):
            acc = final_in[d, group * per_group].astype(F32)
            for at in range(1, per_group):
                acc += final_in[d, group * per_group + at].astype(F32)
            totals.append(acc)
        for part in range(SUB):
            acc = None
            for group in range(groups):
                for slot in range(CAP):
                    at = slot * SUB + part
                    column = group * block_rows + slot * SUB
                    term = table[:, column:column + 1] * totals[group][at:at + 1, :]
                    acc = term if acc is None else acc + term
            routed = acc.astype(BF)
            if d == 0:
                routed_s[:, columns(part)] = routed
            else:
                out_s[:, columns(part)] = (
                    routed_s[:, columns(part)].astype(F32) + routed.astype(F32)
                ).astype(BF)
                out_copy(part).start()

    def out_copy(part):
        return pltpu.make_async_copy(
            out_s.at[:, columns(part)], out_hbm.at[:, columns(part)], out_sem.at[part]
        )

    relay(0)
    for load in up_loads:
        load.wait()
    gathered(0)
    each(chunks, forward_hidden)
    relay(1)
    for load in down_loads + saved_load:
        load.wait()
    partial(0)
    gathered(1)
    each(chunks, backward_hidden)
    pass_on(0)
    partial(1)
    table_f, table_b = route_columns(0), route_columns(1)
    pass_on(1)
    finish(0, table_f)
    finish(1, table_b)

    for d in range(2):
        t_copy(d).wait_send()
        each(high - 1, lambda k, d=d: z_copy(d, k + 1).wait_send())
        each(high, lambda k, d=d: y_copy(d, k, lo).wait_send())
        for n in range(len(cuts)):
            a_copy(d, n).wait_send()
            each(high, lambda k, d=d, n=n: f_copy(d, n, k).wait_send())
    for part in range(SUB):
        out_copy(part).wait()


def solution(mesh):
    sections, ep = mesh.shape["pp"], mesh.shape["ep"]
    groups = ep // SPLIT
    high = ep // PAIR

    def body(x, dy, rf, rb, sf, sb, saved, wg, wu, wd):
        _, tokens, model = x.shape
        topk = rf.shape[2]
        hidden = wg.shape[1]
        width = model // SUB
        block_rows = CAP * SUB
        early = width // 256 * 128 + 128 if width > 256 else width
        lane_chunks = [(0, early), (early, width - early)] if early < width else [(0, width)]
        cuts = len(lane_chunks)
        anywhere = pl.BlockSpec(memory_space=pl.ANY)
        out = pl.pallas_call(
            functools.partial(kernel, (sections, ep), groups, lane_chunks),
            out_shape=jax.ShapeDtypeStruct((tokens, model), BF),
            in_specs=[anywhere] * 10,
            out_specs=anywhere,
            scratch_shapes=[
                pltpu.VMEM((2, SUB * tokens, width), BF),
                pltpu.VMEM((2, topk, tokens), jnp.int32),
                pltpu.VMEM((2, topk, tokens), F32),
                pltpu.VMEM((ep * CAP, 2, hidden), F32),
                pltpu.VMEM((width, SUB * 2 * hidden), BF),
                pltpu.VMEM((SUB * hidden, width), BF),
                pltpu.VMEM((2, groups, block_rows, width), BF),
                pltpu.VMEM((2, high, PAIR, block_rows, width), BF),
                pltpu.VMEM((high, PAIR, block_rows, hidden), BF),
                pltpu.VMEM((high, PAIR, block_rows, 2 * hidden), BF),
                pltpu.VMEM((2, high, block_rows, width), BF),
                pltpu.VMEM((2, high, block_rows, width), F32),
                pltpu.VMEM((2, high, block_rows, width), BF),
                pltpu.VMEM((2, high, block_rows, width), BF),
                pltpu.VMEM((2, high, block_rows, width), BF),
                pltpu.VMEM((2, groups * block_rows, tokens), F32),
                pltpu.VMEM((2, groups * block_rows, tokens), F32),
                pltpu.VMEM((tokens, model), BF),
                pltpu.VMEM((tokens, model), BF),
                pltpu.SemaphoreType.DMA((5 + 5 * SUB,)),
                pltpu.SemaphoreType.DMA((SUB,)),
            ]
            + [pltpu.SemaphoreType.DMA((2, high))] * 4
            + [pltpu.SemaphoreType.DMA((2, cuts))] * 2
            + [pltpu.SemaphoreType.DMA((2, cuts, high))] * 2
            + [pltpu.SemaphoreType.DMA((2,))] * 2,
            compiler_params=pltpu.CompilerParams(
                collective_id=0, has_side_effects=True, vmem_limit_bytes=VMEM_BYTES
            ),
            name="experts",
        )(
            x[0], dy[0], rf[0].T, rb[0].T, sf[0].T, sb[0].T,
            saved.reshape(ep * CAP, 2, hidden), wg, wu, wd,
        )
        return out[None]

    in_specs = (
        P("pp", "ep", None),
        P("pp", "ep", None),
        P("pp", "ep", None),
        P("pp", "ep", None),
        P("pp", "ep", None),
        P("pp", "ep", None),
        P("pp", None, None, None, "ep"),
        P(None, "ep"),
        P(None, "ep"),
        P("ep", None),
    )
    out_specs = P("pp", "ep", None)
    return jax.shard_map(body, mesh=mesh, in_specs=in_specs, out_specs=out_specs, check_vma=False)
```

time: 46 us -> 33.7 us (0.73)
  local copies, waits for them, and re-layouts: 10.4 us -> 2.16 us
  Pallas kernels: 35.2 us -> 31.3 us
    unnamed x18 -> x1, local copies, waits for them, and re-layouts: 10.4 us -> 2.16 us
    pallas_call x2 -> x1, Pallas kernels: 35.2 us -> 31.3 us  [body(): pl.pallas_call(functools.partial(kernel, (sections, ep), groups, lane_chu...]
where the time goes in v2:
time: 33.7 us; the launch traced here: 33.5 us
  Pallas kernels  31.3 us (93%)
  local copies, waits for them, and re-layouts  2.16 us (6%)
    pallas_call x1, Pallas kernels, body(): pl.pallas_call(functools.partial(kernel, (sections, ep), groups, lane_chu...  31.3 us
    unnamed x1, local copies, waits for them, and re-layouts  2.16 us

profile of v2, /device:TPU:1, one launch (start us, length us, event | category | flops | bytes accessed | tf_op | source)
XLA Modules:
  0.0 33.5 jit_solution(6326546797884248922)
XLA Ops:
  0.0 31.3 %experts.1 = bf16[64,7168]{1,0:T(8,128)(2,1)} custom-call(bf16[64,7168]{1,0:T(8,128)(2,1)} %bitcast.17, bf16[64,7168]{1,0:T(8,128)(2,1)} %bitcast.18, s32[8,64]{1,0:T(8,128)} %bitcast.20, s32[8,64]{1,0:T(8,128)} %bitcast.21, f32[8,64]{1,0:T(8,128)} %bitcast.22, f32[8,64]{1,0:T(8,128)} %bitcast.23, f32[16,2,128]{2,1,0:T(2,128)} %bitcast.19, ...), custom_call_target="tpu_custom_call" | custom-call | tf_op jit(solution)/shard_map/experts/pallas_call | solution.py:377
  31.3 2.2 %copy.12 = bf16[1,64,7168]{2,1,0:T(8,128)(2,1)} copy(bf16[1,64,7168]{2,1,0:T(8,128)(2,1)} %bitcast.16) | data formatting | bytes 1835008

commit v3 on v2

--- a/solution.py
+++ b/solution.py
@@ -62,8 +62,8 @@
     x_hbm, dy_hbm, rf_hbm, rb_hbm, sf_hbm, sb_hbm, saved_hbm, wg_hbm, wu_hbm, wd_hbm,
     out_hbm,
     tokens_s, route_s, score_s, saved_s, wgu_s, wd_s,
-    slots, rows, hid, grad, away, mine, pair_in, pair_out, final_in, table_s, table_in, routed_s, out_s,
-    load_sem, out_sem, z_send, z_recv, y_send, y_recv, a_send, a_recv, f_send, f_recv, t_send, t_recv,
+    saved_in, slots, rows, hid, grad, parts_s, away, mine, pair_in, pair_out, final_in, table_s, table_in, routed_s, out_s,
+    load_sem, out_sem, z_send, z_recv, y_send, y_recv, a_send, a_recv, f_send, f_recv, t_send, t_recv, s_send, s_recv,
 ):
     sections, ep = axes
     high = ep // PAIR
@@ -77,6 +77,8 @@
     other = 1 - lo
     after, before = lax.rem(p + 1, sections), lax.rem(p + sections - 1, sections)
     ahead = (after, before)
+    works_for = (p, before)
+    gives_to = (after, p)
 
     def columns(part):
         return pl.ds(part * width, width)
@@ -143,7 +145,7 @@
         to = lax.rem(hi + k, high)
         return pltpu.make_async_remote_copy(
             slots.at[d, to // per_group], rows.at[d, hi, lo],
-            z_send.at[d, k], z_recv.at[d, k], (p, to * PAIR + lo), MESH,
+            z_send.at[d, k], z_recv.at[d, k], (works_for[d], to * PAIR + lo), MESH,
         )
 
     def y_copy(d, k, side):
@@ -152,6 +154,8 @@
             rows.at[d, block, side], rows.at[d, block, side],
             y_send.at[d, k], y_recv.at[d, k], (p, hi * PAIR + other), MESH,
         )
+
+    saved_copy = pltpu.make_async_remote_copy(saved_s, saved_in, s_send, s_recv, (before, e), MESH)
 
     def t_copy(d):
         return pltpu.make_async_remote_copy(
@@ -173,23 +177,19 @@
             slots[d, group] = jnp.dot(
                 chosen[group], tokens_s[d], preferred_element_type=F32
             ).astype(BF)
-        rows[d, hi, lo] = slots[d, hi // per_group]
 
     pick(0)
+    rows[0, hi, lo] = slots[0, hi // per_group]
     pl.semaphore_wait(barrier, PAIR - 1 + 3 * high - 1)
-    for d in range(2):
-        if d:
-            pick(d)
-        each(high - 1, lambda k, d=d: z_copy(d, k + 1).start())
-        y_copy(d, 0, lo).start()
-    for d in range(2):
-        t_copy(d).start()
+    each(high - 1, lambda k: z_copy(0, k + 1).start())
+    y_copy(0, 0, lo).start()
+    pick(1)
 
     def relay(d):
         def step(k):
-            z_copy(d, k + 1).wait_recv()
-            y_copy(d, k + 1, lo).start()
-        each(high - 1, step)
+            z_copy(d, k + 1 - d).wait_recv()
+            y_copy(d, k + 1 - d, lo).start()
+        each(high - 1 + d, step)
 
     def gathered(d):
         each(high, lambda k: y_copy(d, k, other).wait_recv())
@@ -231,7 +231,7 @@
             )
         grad_hidden = spread(acc)
         size = step_high * PAIR * CAP
-        kept = saved_s[pl.ds(chunk * size, size)]
+        kept = saved_in[pl.ds(chunk * size, size)]
         gate = jnp.broadcast_to(kept[:, 0:1, :], (size, SUB, hidden)).reshape(full, hidden)
         up = jnp.broadcast_to(kept[:, 1:2, :], (size, SUB, hidden)).reshape(full, hidden)
         sigma = 1.0 / (1.0 + jnp.exp(-gate))
@@ -242,13 +242,17 @@
 
     def side_parts(source, chunk):
         held = jnp.concatenate([source[at_chunk(chunk), other], source[at_chunk(chunk), lo]], axis=0)
-        return jnp.concatenate([masked(held, mask) for mask in masks(held.shape[-1])], axis=1)
+        wide = held.shape[-1]
+        for part, mask in enumerate(masks(wide)):
+            parts_s[pl.ds(chunk * full, full), pl.ds(part * wide, wide)] = masked(held, mask)
 
     def forward_out(chunk, cut):
-        return jnp.dot(side_parts(hid, chunk), wd_s[:, cut], preferred_element_type=F32)
+        held = parts_s[pl.ds(chunk * full, full), pl.ds(0, SUB * hidden)]
+        return jnp.dot(held, wd_s[:, cut], preferred_element_type=F32)
 
     def backward_out(chunk, cut):
-        return lax.dot_general(side_parts(grad, chunk), wgu_s[cut, :], NT, preferred_element_type=F32)
+        held = parts_s[pl.ds(chunk * full, full), :]
+        return lax.dot_general(held, wgu_s[cut, :], NT, preferred_element_type=F32)
 
     outs = (forward_out, backward_out)
     cuts = [pl.ds(low, size) for low, size in lane_chunks]
@@ -264,10 +268,11 @@
         slot = block if arriving else hi
         return pltpu.make_async_remote_copy(
             pair_out.at[d, block, :, cuts[n]], final_in.at[d, slot, :, cuts[n]],
-            f_send.at[d, n, k], f_recv.at[d, n, k], (ahead[d], block * PAIR + lo), MESH,
+            f_send.at[d, n, k], f_recv.at[d, n, k], (gives_to[d], block * PAIR + lo), MESH,
         )
 
     def partial(d):
+        each(chunks, lambda chunk: side_parts((hid, grad)[d], chunk))
         for n, cut in enumerate(cuts):
             def make(chunk, cut=cut):
                 value = outs[d](chunk, cut)
@@ -281,13 +286,16 @@
         for n, cut in enumerate(cuts):
             a_copy(d, n).wait_recv()
 
-            def add(k, n=n, cut=cut):
-                block = lax.rem(hi + k, high)
-                pair_out[d, block, :, cut] = (
-                    mine[d, block, :, cut] + pair_in[d, block, :, cut].astype(F32)
-                ).astype(BF)
-                f_copy(d, n, k).start()
-            each(high, add)
+            def add(block, cut=cut):
+                return (mine[d, block, :, cut] + pair_in[d, block, :, cut].astype(F32)).astype(BF)
+
+            def send(k, n=n, cut=cut):
+                block = lax.rem(hi + k + d, high)
+                pair_out[d, block, :, cut] = add(block)
+                f_copy(d, n, k + d).start()
+            each(high - d, send)
+            if d:
+                final_in[d, hi, :, cut] = add(hi)
 
     def route_columns(d):
         t_copy(d).wait_recv()
@@ -301,7 +309,7 @@
 
     def finish(d, table):
         for n in range(len(cuts)):
-            each(high, lambda k, n=n: f_copy(d, n, k, True).wait_recv())
+            each(high - d, lambda k, n=n: f_copy(d, n, k + d, True).wait_recv())
         totals = []
         for group in range(groups):
             acc = final_in[d, group * per_group].astype(F32)
@@ -331,15 +339,22 @@
         )
 
     relay(0)
+    for load in saved_load:
+        load.wait()
+    each(high, lambda k: z_copy(1, k).start())
+    saved_copy.start()
+    for d in range(2):
+        t_copy(d).start()
     for load in up_loads:
         load.wait()
     gathered(0)
     each(chunks, forward_hidden)
     relay(1)
-    for load in down_loads + saved_load:
+    for load in down_loads:
         load.wait()
     partial(0)
     gathered(1)
+    saved_copy.wait_recv()
     each(chunks, backward_hidden)
     pass_on(0)
     partial(1)
@@ -350,13 +365,28 @@
 
     for d in range(2):
         t_copy(d).wait_send()
-        each(high - 1, lambda k, d=d: z_copy(d, k + 1).wait_send())
+        each(high - 1 + d, lambda k, d=d: z_copy(d, k + 1 - d).wait_send())
         each(high, lambda k, d=d: y_copy(d, k, lo).wait_send())
         for n in range(len(cuts)):
             a_copy(d, n).wait_send()
-            each(high, lambda k, d=d, n=n: f_copy(d, n, k).wait_send())
+            each(high - d, lambda k, d=d, n=n: f_copy(d, n, k + d).wait_send())
+    saved_copy.wait_send()
     for part in range(SUB):
         out_copy(part).wait()
+
+
+def write_kernel(value_hbm, out_hbm, sem):
+    tokens, model = value_hbm.shape
+    high, wide = tokens // sem.shape[0], model // sem.shape[1]
+    copies = []
+    for at in range(sem.shape[0]):
+        for side in range(sem.shape[1]):
+            place = (pl.ds(at * high, high), pl.ds(side * wide, wide))
+            copies.append(pltpu.make_async_copy(value_hbm.at[place], out_hbm.at[place], sem.at[at, side]))
+    for copy in copies:
+        copy.start()
+    for copy in copies:
+        copy.wait()
 
 
 def solution(mesh):
@@ -370,8 +400,7 @@
         hidden = wg.shape[1]
         width = model // SUB
         block_rows = CAP * SUB
-        early = width // 256 * 128 + 128 if width > 256 else width
-        lane_chunks = [(0, early), (early, width - early)] if early < width else [(0, width)]
+        lane_chunks = [(low, min(256, width - low)) for low in range(0, width, 256)]
         cuts = len(lane_chunks)
         anywhere = pl.BlockSpec(memory_space=pl.ANY)
         out = pl.pallas_call(
@@ -386,10 +415,12 @@
                 pltpu.VMEM((ep * CAP, 2, hidden), F32),
                 pltpu.VMEM((width, SUB * 2 * hidden), BF),
                 pltpu.VMEM((SUB * hidden, width), BF),
+                pltpu.VMEM((ep * CAP, 2, hidden), F32),
                 pltpu.VMEM((2, groups, block_rows, width), BF),
                 pltpu.VMEM((2, high, PAIR, block_rows, width), BF),
                 pltpu.VMEM((high, PAIR, block_rows, hidden), BF),
                 pltpu.VMEM((high, PAIR, block_rows, 2 * hidden), BF),
+                pltpu.VMEM((ep * block_rows, SUB * 2 * hidden), BF),
                 pltpu.VMEM((2, high, block_rows, width), BF),
                 pltpu.VMEM((2, high, block_rows, width), F32),
                 pltpu.VMEM((2, high, block_rows, width), BF),
@@ -405,7 +436,8 @@
             + [pltpu.SemaphoreType.DMA((2, high))] * 4
             + [pltpu.SemaphoreType.DMA((2, cuts))] * 2
             + [pltpu.SemaphoreType.DMA((2, cuts, high))] * 2
-            + [pltpu.SemaphoreType.DMA((2,))] * 2,
+            + [pltpu.SemaphoreType.DMA((2,))] * 2
+            + [pltpu.SemaphoreType.DMA] * 2,
             compiler_params=pltpu.CompilerParams(
                 collective_id=0, has_side_effects=True, vmem_limit_bytes=VMEM_BYTES
             ),
@@ -414,6 +446,15 @@
             x[0], dy[0], rf[0].T, rb[0].T, sf[0].T, sb[0].T,
             saved.reshape(ep * CAP, 2, hidden), wg, wu, wd,
         )
+        out = pl.pallas_call(
+            write_kernel,
+            out_shape=jax.ShapeDtypeStruct((tokens, model), BF),
+            in_specs=[anywhere],
+            out_specs=anywhere,
+            scratch_shapes=[pltpu.SemaphoreType.DMA((tokens // block_rows, 2))],
+            compiler_params=pltpu.CompilerParams(vmem_limit_bytes=VMEM_BYTES),
+            name="write",
+        )(out)
         return out[None]
 
     in_specs = (

time: 33.7 us -> 62.4 us (1.85)
  the two profiles are of different devices: /device:TPU:1 before, /device:TPU:0 now
where the time goes in v3:
time: 62.4 us; the launch traced here: 62.2 us
  Pallas kernels  62.2 us (100%)
    pallas_call x1, Pallas kernels, body(): pl.pallas_call(functools.partial(kernel, (sections, ep), groups, lane_chu...  33.2 us
    pallas_call x1, Pallas kernels, body(): pl.pallas_call(write_kernel, out_shape=jax.ShapeDtypeStruct((tokens, mode...  29 us

profile of v3, /device:TPU:0, one launch (start us, length us, event | category | flops | bytes accessed | tf_op | source)
XLA Modules:
  0.0 62.2 jit_solution(7567138176372339235)
XLA Ops:
  0.0 33.2 %experts.1.value_hbm = bf16[64,7168]{1,0:T(8,128)(2,1)} custom-call(bf16[64,7168]{1,0:T(8,128)(2,1)} %bitcast.16, bf16[64,7168]{1,0:T(8,128)(2,1)} %bitcast.17, s32[8,64]{1,0:T(8,128)} %bitcast.19, s32[8,64]{1,0:T(8,128)} %bitcast.20, f32[8,64]{1,0:T(8,128)} %bitcast.21, f32[8,64]{1,0:T(8,128)} %bitcast.22, f32[16,2,128]{2,1,0:T(2,128)} %bitcast.18, ...), custom_call_target="tpu_custom_call" | custom-call | tf_op jit(solution)/shard_map/experts/pallas_call | solution.py:406
  33.2 29.0 %write.1 = bf16[64,7168]{1,0:T(8,128)(2,1)} custom-call(bf16[64,7168]{1,0:T(8,128)(2,1)} %experts.1.value_hbm), custom_call_target="tpu_custom_call" | custom-call | tf_op jit(solution)/shard_map/write/pallas_call | solution.py:449

commit v4 on v3

--- a/solution.py
+++ b/solution.py
@@ -130,7 +130,7 @@
     each(high, lambda k: greet(after, lax.rem(hi + k, high) * PAIR + lo))
     each(high, lambda k: greet(before, lax.rem(hi + k, high) * PAIR + lo))
 
-    for load in inputs[1] + up_loads + down_loads + saved_load:
+    for load in inputs[1]:
         load.start()
 
     for load in small:
@@ -183,7 +183,13 @@
     pl.semaphore_wait(barrier, PAIR - 1 + 3 * high - 1)
     each(high - 1, lambda k: z_copy(0, k + 1).start())
     y_copy(0, 0, lo).start()
+    for load in saved_load + up_loads + down_loads:
+        load.start()
     pick(1)
+    each(high, lambda k: z_copy(1, k).start())
+    for load in saved_load:
+        load.wait()
+    saved_copy.start()
 
     def relay(d):
         def step(k):
@@ -339,10 +345,6 @@
         )
 
     relay(0)
-    for load in saved_load:
-        load.wait()
-    each(high, lambda k: z_copy(1, k).start())
-    saved_copy.start()
     for d in range(2):
         t_copy(d).start()
     for load in up_loads:
@@ -375,18 +377,19 @@
         out_copy(part).wait()
 
 
-def write_kernel(value_hbm, out_hbm, sem):
-    tokens, model = value_hbm.shape
-    high, wide = tokens // sem.shape[0], model // sem.shape[1]
-    copies = []
-    for at in range(sem.shape[0]):
-        for side in range(sem.shape[1]):
-            place = (pl.ds(at * high, high), pl.ds(side * wide, wide))
-            copies.append(pltpu.make_async_copy(value_hbm.at[place], out_hbm.at[place], sem.at[at, side]))
-    for copy in copies:
-        copy.start()
-    for copy in copies:
-        copy.wait()
+def write_kernel(value_hbm, out_hbm, held, load_sem, store_sem):
+    wide = value_hbm.shape[1] // SUB
+    loads, stores = [], []
+    for at in range(SUB):
+        place = (slice(None), pl.ds(at * wide, wide))
+        loads.append(pltpu.make_async_copy(value_hbm.at[place], held.at[at], load_sem.at[at]))
+        stores.append(pltpu.make_async_copy(held.at[at], out_hbm.at[place], store_sem.at[at]))
+        loads[at].start()
+    for at in range(SUB):
+        loads[at].wait()
+        stores[at].start()
+    for store in stores:
+        store.wait()
 
 
 def solution(mesh):
@@ -451,7 +454,11 @@
             out_shape=jax.ShapeDtypeStruct((tokens, model), BF),
             in_specs=[anywhere],
             out_specs=anywhere,
-            scratch_shapes=[pltpu.SemaphoreType.DMA((tokens // block_rows, 2))],
+            scratch_shapes=[
+                pltpu.VMEM((SUB, tokens, width), BF),
+                pltpu.SemaphoreType.DMA((SUB,)),
+                pltpu.SemaphoreType.DMA((SUB,)),
+            ],
             compiler_params=pltpu.CompilerParams(vmem_limit_bytes=VMEM_BYTES),
             name="write",
         )(out)

time: 62.4 us -> 35.2 us (0.56)
  Pallas kernels: 62.2 us -> 35 us
    pallas_call x1, Pallas kernels: 29 us -> 2.04 us  [body(): pl.pallas_call(write_kernel, out_shape=jax.ShapeDtypeStruct((tokens, mode...]
where the time goes in v4:
time: 35.2 us; the launch traced here: 35 us
  Pallas kernels  35 us (99%)
    pallas_call x1, Pallas kernels, body(): pl.pallas_call(functools.partial(kernel, (sections, ep), groups, lane_chu...  33 us
    pallas_call x1, Pallas kernels, body(): pl.pallas_call(write_kernel, out_shape=jax.ShapeDtypeStruct((tokens, mode...  2.04 us

profile of v4, /device:TPU:0, one launch (start us, length us, event | category | flops | bytes accessed | tf_op | source)
XLA Modules:
  0.0 35.0 jit_solution(15758446034689251674)
XLA Ops:
  0.0 33.0 %experts.1.value_hbm = bf16[64,7168]{1,0:T(8,128)(2,1)} custom-call(bf16[64,7168]{1,0:T(8,128)(2,1)} %bitcast.16, bf16[64,7168]{1,0:T(8,128)(2,1)} %bitcast.17, s32[8,64]{1,0:T(8,128)} %bitcast.19, s32[8,64]{1,0:T(8,128)} %bitcast.20, f32[8,64]{1,0:T(8,128)} %bitcast.21, f32[8,64]{1,0:T(8,128)} %bitcast.22, f32[16,2,128]{2,1,0:T(2,128)} %bitcast.18, ...), custom_call_target="tpu_custom_call" | custom-call | tf_op jit(solution)/shard_map/experts/pallas_call | solution.py:409
  33.0 2.0 %write.1 = bf16[64,7168]{1,0:T(8,128)(2,1)} custom-call(bf16[64,7168]{1,0:T(8,128)(2,1)} %experts.1.value_hbm), custom_call_target="tpu_custom_call" | custom-call | tf_op jit(solution)/shard_map/write/pallas_call | solution.py:452

commit v5 on v4

--- a/solution.py
+++ b/solution.py
@@ -62,8 +62,8 @@
     x_hbm, dy_hbm, rf_hbm, rb_hbm, sf_hbm, sb_hbm, saved_hbm, wg_hbm, wu_hbm, wd_hbm,
     out_hbm,
     tokens_s, route_s, score_s, saved_s, wgu_s, wd_s,
-    saved_in, slots, rows, hid, grad, parts_s, away, mine, pair_in, pair_out, final_in, table_s, table_in, routed_s, out_s,
-    load_sem, out_sem, z_send, z_recv, y_send, y_recv, a_send, a_recv, f_send, f_recv, t_send, t_recv, s_send, s_recv,
+    saved_in, slots, shifted, total_s, total_in, rows, hid, grad, parts_s, away, mine, pair_in, pair_out, final_in, table_s, table_in, routed_s, out_s,
+    load_sem, out_sem, z_send, z_recv, y_send, y_recv, a_send, a_recv, f_send, f_recv, t_send, t_recv, s_send, s_recv, x_send, x_recv,
 ):
     sections, ep = axes
     high = ep // PAIR
@@ -77,8 +77,6 @@
     other = 1 - lo
     after, before = lax.rem(p + 1, sections), lax.rem(p + sections - 1, sections)
     ahead = (after, before)
-    works_for = (p, before)
-    gives_to = (after, p)
 
     def columns(part):
         return pl.ds(part * width, width)
@@ -127,8 +125,8 @@
 
     greet(p, hi * PAIR + other)
     each(high - 1, lambda k: greet(p, lax.rem(hi + k + 1, high) * PAIR + lo))
-    each(high, lambda k: greet(after, lax.rem(hi + k, high) * PAIR + lo))
-    each(high, lambda k: greet(before, lax.rem(hi + k, high) * PAIR + lo))
+    greet(after, e)
+    greet(before, e)
 
     for load in inputs[1]:
         load.start()
@@ -143,9 +141,10 @@
 
     def z_copy(d, k):
         to = lax.rem(hi + k, high)
+        source = shifted if d else slots.at[0]
         return pltpu.make_async_remote_copy(
-            slots.at[d, to // per_group], rows.at[d, hi, lo],
-            z_send.at[d, k], z_recv.at[d, k], (works_for[d], to * PAIR + lo), MESH,
+            source.at[to // per_group], rows.at[d, hi, lo],
+            z_send.at[d, k], z_recv.at[d, k], (p, to * PAIR + lo), MESH,
         )
 
     def y_copy(d, k, side):
@@ -155,6 +154,12 @@
             y_send.at[d, k], y_recv.at[d, k], (p, hi * PAIR + other), MESH,
         )
 
+    shift_copy = pltpu.make_async_remote_copy(
+        slots.at[1], shifted, x_send.at[1], x_recv.at[1], (before, e), MESH
+    )
+    total_copy = pltpu.make_async_remote_copy(
+        total_s, total_in, x_send.at[0], x_recv.at[0], (after, e), MESH
+    )
     saved_copy = pltpu.make_async_remote_copy(saved_s, saved_in, s_send, s_recv, (before, e), MESH)
 
     def t_copy(d):
@@ -180,22 +185,26 @@
 
     pick(0)
     rows[0, hi, lo] = slots[0, hi // per_group]
-    pl.semaphore_wait(barrier, PAIR - 1 + 3 * high - 1)
+    pl.semaphore_wait(barrier, PAIR - 1 + high - 1 + 2)
     each(high - 1, lambda k: z_copy(0, k + 1).start())
     y_copy(0, 0, lo).start()
     for load in saved_load + up_loads + down_loads:
         load.start()
     pick(1)
-    each(high, lambda k: z_copy(1, k).start())
+    shift_copy.start()
     for load in saved_load:
         load.wait()
     saved_copy.start()
+    shift_copy.wait_recv()
+    rows[1, hi, lo] = shifted[hi // per_group]
+    each(high - 1, lambda k: z_copy(1, k + 1).start())
+    y_copy(1, 0, lo).start()
 
     def relay(d):
         def step(k):
-            z_copy(d, k + 1 - d).wait_recv()
-            y_copy(d, k + 1 - d, lo).start()
-        each(high - 1 + d, step)
+            z_copy(d, k + 1).wait_recv()
+            y_copy(d, k + 1, lo).start()
+        each(high - 1, step)
 
     def gathered(d):
         each(high, lambda k: y_copy(d, k, other).wait_recv())
@@ -274,7 +283,7 @@
         slot = block if arriving else hi
         return pltpu.make_async_remote_copy(
             pair_out.at[d, block, :, cuts[n]], final_in.at[d, slot, :, cuts[n]],
-            f_send.at[d, n, k], f_recv.at[d, n, k], (gives_to[d], block * PAIR + lo), MESH,
+            f_send.at[d, n, k], f_recv.at[d, n, k], (p, block * PAIR + lo), MESH,
         )
 
     def partial(d):
@@ -296,12 +305,11 @@
                 return (mine[d, block, :, cut] + pair_in[d, block, :, cut].astype(F32)).astype(BF)
 
             def send(k, n=n, cut=cut):
-                block = lax.rem(hi + k + d, high)
+                block = lax.rem(hi + k + 1, high)
                 pair_out[d, block, :, cut] = add(block)
-                f_copy(d, n, k + d).start()
-            each(high - d, send)
-            if d:
-                final_in[d, hi, :, cut] = add(hi)
+                f_copy(d, n, k + 1).start()
+            each(high - 1, send)
+            final_in[d, hi, :, cut] = add(hi)
 
     def route_columns(d):
         t_copy(d).wait_recv()
@@ -313,15 +321,18 @@
             precision=lax.Precision.HIGHEST, preferred_element_type=F32,
         )
 
-    def finish(d, table):
+    def total(d):
         for n in range(len(cuts)):
-            each(high - d, lambda k, n=n: f_copy(d, n, k + d, True).wait_recv())
-        totals = []
+            each(high - 1, lambda k, n=n: f_copy(d, n, k + 1, True).wait_recv())
+        sums = []
         for group in range(groups):
             acc = final_in[d, group * per_group].astype(F32)
             for at in range(1, per_group):
                 acc += final_in[d, group * per_group + at].astype(F32)
-            totals.append(acc)
+            sums.append(acc)
+        return sums
+
+    def finish(d, table, totals):
         for part in range(SUB):
             acc = None
             for group in range(groups):
@@ -361,18 +372,23 @@
     pass_on(0)
     partial(1)
     table_f, table_b = route_columns(0), route_columns(1)
+    for group, value in enumerate(total(0)):
+        total_s[pl.ds(group * block_rows, block_rows), :] = value
+    total_copy.start()
     pass_on(1)
-    finish(0, table_f)
-    finish(1, table_b)
+    total_copy.wait_recv()
+    finish(0, table_f, [total_in[pl.ds(group * block_rows, block_rows), :] for group in range(groups)])
+    finish(1, table_b, total(1))
 
     for d in range(2):
         t_copy(d).wait_send()
-        each(high - 1 + d, lambda k, d=d: z_copy(d, k + 1 - d).wait_send())
+        each(high - 1, lambda k, d=d: z_copy(d, k + 1).wait_send())
         each(high, lambda k, d=d: y_copy(d, k, lo).wait_send())
         for n in range(len(cuts)):
             a_copy(d, n).wait_send()
-            each(high - d, lambda k, d=d, n=n: f_copy(d, n, k + d).wait_send())
-    saved_copy.wait_send()
+            each(high - 1, lambda k, d=d, n=n: f_copy(d, n, k + 1).wait_send())
+    for copy in (saved_copy, shift_copy, total_copy):
+        copy.wait_send()
     for part in range(SUB):
         out_copy(part).wait()
 
@@ -403,7 +419,7 @@
         hidden = wg.shape[1]
         width = model // SUB
         block_rows = CAP * SUB
-        lane_chunks = [(low, min(256, width - low)) for low in range(0, width, 256)]
+        lane_chunks = [(low, min(512, width - low)) for low in range(0, width, 512)]
         cuts = len(lane_chunks)
         anywhere = pl.BlockSpec(memory_space=pl.ANY)
         out = pl.pallas_call(
@@ -420,6 +436,9 @@
                 pltpu.VMEM((SUB * hidden, width), BF),
                 pltpu.VMEM((ep * CAP, 2, hidden), F32),
                 pltpu.VMEM((2, groups, block_rows, width), BF),
+                pltpu.VMEM((groups, block_rows, width), BF),
+                pltpu.VMEM((groups * block_rows, width), F32),
+                pltpu.VMEM((groups * block_rows, width), F32),
                 pltpu.VMEM((2, high, PAIR, block_rows, width), BF),
                 pltpu.VMEM((high, PAIR, block_rows, hidden), BF),
                 pltpu.VMEM((high, PAIR, block_rows, 2 * hidden), BF),
@@ -440,7 +459,8 @@
             + [pltpu.SemaphoreType.DMA((2, cuts))] * 2
             + [pltpu.SemaphoreType.DMA((2, cuts, high))] * 2
             + [pltpu.SemaphoreType.DMA((2,))] * 2
-            + [pltpu.SemaphoreType.DMA] * 2,
+            + [pltpu.SemaphoreType.DMA] * 2
+            + [pltpu.SemaphoreType.DMA((2,))] * 2,
             compiler_params=pltpu.CompilerParams(
                 collective_id=0, has_side_effects=True, vmem_limit_bytes=VMEM_BYTES
             ),

time: 35.2 us -> 33 us (0.937)
  Pallas kernels: 35 us -> 32.8 us
    pallas_call x1, Pallas kernels: 33 us -> 30.7 us  [body(): pl.pallas_call(functools.partial(kernel, (sections, ep), groups, lane_chu...]
where the time goes in v5:
time: 33 us; the launch traced here: 32.8 us
  Pallas kernels  32.8 us (99%)
    pallas_call x1, Pallas kernels, body(): pl.pallas_call(functools.partial(kernel, (sections, ep), groups, lane_chu...  30.7 us
    pallas_call x1, Pallas kernels, body(): pl.pallas_call(write_kernel, out_shape=jax.ShapeDtypeStruct((tokens, mode...  2.04 us

profile of v5, /device:TPU:0, one launch (start us, length us, event | category | flops | bytes accessed | tf_op | source)
XLA Modules:
  0.0 32.8 jit_solution(16503590216248154309)
XLA Ops:
  0.0 30.7 %experts.1.value_hbm = bf16[64,7168]{1,0:T(8,128)(2,1)} custom-call(bf16[64,7168]{1,0:T(8,128)(2,1)} %bitcast.16, bf16[64,7168]{1,0:T(8,128)(2,1)} %bitcast.17, s32[8,64]{1,0:T(8,128)} %bitcast.19, s32[8,64]{1,0:T(8,128)} %bitcast.20, f32[8,64]{1,0:T(8,128)} %bitcast.21, f32[8,64]{1,0:T(8,128)} %bitcast.22, f32[16,2,128]{2,1,0:T(2,128)} %bitcast.18, ...), custom_call_target="tpu_custom_call" | custom-call | tf_op jit(solution)/shard_map/experts/pallas_call | solution.py:425
  30.7 2.0 %write.1 = bf16[64,7168]{1,0:T(8,128)(2,1)} custom-call(bf16[64,7168]{1,0:T(8,128)(2,1)} %experts.1.value_hbm), custom_call_target="tpu_custom_call" | custom-call | tf_op jit(solution)/shard_map/write/pallas_call | solution.py:472

commit v6 on v5

--- a/solution.py
+++ b/solution.py
@@ -184,21 +184,14 @@
             ).astype(BF)
 
     pick(0)
+    pick(1)
     rows[0, hi, lo] = slots[0, hi // per_group]
     pl.semaphore_wait(barrier, PAIR - 1 + high - 1 + 2)
     each(high - 1, lambda k: z_copy(0, k + 1).start())
     y_copy(0, 0, lo).start()
+    shift_copy.start()
     for load in saved_load + up_loads + down_loads:
         load.start()
-    pick(1)
-    shift_copy.start()
-    for load in saved_load:
-        load.wait()
-    saved_copy.start()
-    shift_copy.wait_recv()
-    rows[1, hi, lo] = shifted[hi // per_group]
-    each(high - 1, lambda k: z_copy(1, k + 1).start())
-    y_copy(1, 0, lo).start()
 
     def relay(d):
         def step(k):
@@ -356,6 +349,13 @@
         )
 
     relay(0)
+    shift_copy.wait_recv()
+    rows[1, hi, lo] = shifted[hi // per_group]
+    each(high - 1, lambda k: z_copy(1, k + 1).start())
+    y_copy(1, 0, lo).start()
+    for load in saved_load:
+        load.wait()
+    saved_copy.start()
     for d in range(2):
         t_copy(d).start()
     for load in up_loads:

time: 33 us -> 32.5 us (0.985)
  Pallas kernels: 32.8 us -> 32.3 us
    pallas_call x1, Pallas kernels: 30.7 us -> 30.2 us  [body(): pl.pallas_call(functools.partial(kernel, (sections, ep), groups, lane_chu...]
where the time goes in v6:
time: 32.5 us; the launch traced here: 32.3 us
  Pallas kernels  32.3 us (99%)
    pallas_call x1, Pallas kernels, body(): pl.pallas_call(functools.partial(kernel, (sections, ep), groups, lane_chu...  30.2 us
    pallas_call x1, Pallas kernels, body(): pl.pallas_call(write_kernel, out_shape=jax.ShapeDtypeStruct((tokens, mode...  2.04 us

profile of v6, /device:TPU:0, one launch (start us, length us, event | category | flops | bytes accessed | tf_op | source)
XLA Modules:
  0.0 32.3 jit_solution(2882041906276007357)
XLA Ops:
  0.0 30.2 %experts.1.value_hbm = bf16[64,7168]{1,0:T(8,128)(2,1)} custom-call(bf16[64,7168]{1,0:T(8,128)(2,1)} %bitcast.16, bf16[64,7168]{1,0:T(8,128)(2,1)} %bitcast.17, s32[8,64]{1,0:T(8,128)} %bitcast.19, s32[8,64]{1,0:T(8,128)} %bitcast.20, f32[8,64]{1,0:T(8,128)} %bitcast.21, f32[8,64]{1,0:T(8,128)} %bitcast.22, f32[16,2,128]{2,1,0:T(2,128)} %bitcast.18, ...), custom_call_target="tpu_custom_call" | custom-call | tf_op jit(solution)/shard_map/experts/pallas_call | solution.py:425
  30.2 2.0 %write.1 = bf16[64,7168]{1,0:T(8,128)(2,1)} custom-call(bf16[64,7168]{1,0:T(8,128)(2,1)} %experts.1.value_hbm), custom_call_target="tpu_custom_call" | custom-call | tf_op jit(solution)/shard_map/write/pallas_call | solution.py:472

commit v7 on v6

--- a/solution.py
+++ b/solution.py
@@ -335,7 +335,7 @@
                     term = table[:, column:column + 1] * totals[group][at:at + 1, :]
                     acc = term if acc is None else acc + term
             routed = acc.astype(BF)
-            if d == 0:
+            if d == 1:
                 routed_s[:, columns(part)] = routed
             else:
                 out_s[:, columns(part)] = (
@@ -373,12 +373,14 @@
     partial(1)
     table_f, table_b = route_columns(0), route_columns(1)
     for group, value in enumerate(total(0)):
-        total_s[pl.ds(group * block_rows, block_rows), :] = value
+        total_s[pl.ds(group * block_rows, block_rows), :] = value.astype(BF)
     total_copy.start()
     pass_on(1)
+    finish(1, table_b, total(1))
     total_copy.wait_recv()
-    finish(0, table_f, [total_in[pl.ds(group * block_rows, block_rows), :] for group in range(groups)])
-    finish(1, table_b, total(1))
+    finish(0, table_f, [
+        total_in[pl.ds(group * block_rows, block_rows), :].astype(F32) for group in range(groups)
+    ])
 
     for d in range(2):
         t_copy(d).wait_send()
@@ -437,8 +439,8 @@
                 pltpu.VMEM((ep * CAP, 2, hidden), F32),
                 pltpu.VMEM((2, groups, block_rows, width), BF),
                 pltpu.VMEM((groups, block_rows, width), BF),
-                pltpu.VMEM((groups * block_rows, width), F32),
-                pltpu.VMEM((groups * block_rows, width), F32),
+                pltpu.VMEM((groups * block_rows, width), BF),
+                pltpu.VMEM((groups * block_rows, width), BF),
                 pltpu.VMEM((2, high, PAIR, block_rows, width), BF),
                 pltpu.VMEM((high, PAIR, block_rows, hidden), BF),
                 pltpu.VMEM((high, PAIR, block_rows, 2 * hidden), BF),

time: 32.5 us -> 32.8 us (level)
    pallas_call x1, Pallas kernels: 30.2 us -> 30.6 us  [body(): pl.pallas_call(functools.partial(kernel, (sections, ep), groups, lane_chu...]
where the time goes in v7:
time: 32.8 us; the launch traced here: 32.6 us
  Pallas kernels  32.6 us (99%)
    pallas_call x1, Pallas kernels, body(): pl.pallas_call(functools.partial(kernel, (sections, ep), groups, lane_chu...  30.6 us
    pallas_call x1, Pallas kernels, body(): pl.pallas_call(write_kernel, out_shape=jax.ShapeDtypeStruct((tokens, mode...  2.04 us

profile of v7, /device:TPU:0, one launch (start us, length us, event | category | flops | bytes accessed | tf_op | source)
XLA Modules:
  0.0 32.6 jit_solution(1716177116183828074)
XLA Ops:
  0.0 30.6 %experts.1.value_hbm = bf16[64,7168]{1,0:T(8,128)(2,1)} custom-call(bf16[64,7168]{1,0:T(8,128)(2,1)} %bitcast.16, bf16[64,7168]{1,0:T(8,128)(2,1)} %bitcast.17, s32[8,64]{1,0:T(8,128)} %bitcast.19, s32[8,64]{1,0:T(8,128)} %bitcast.20, f32[8,64]{1,0:T(8,128)} %bitcast.21, f32[8,64]{1,0:T(8,128)} %bitcast.22, f32[16,2,128]{2,1,0:T(2,128)} %bitcast.18, ...), custom_call_target="tpu_custom_call" | custom-call | tf_op jit(solution)/shard_map/experts/pallas_call | solution.py:427
  30.6 2.0 %write.1 = bf16[64,7168]{1,0:T(8,128)(2,1)} custom-call(bf16[64,7168]{1,0:T(8,128)(2,1)} %experts.1.value_hbm), custom_call_target="tpu_custom_call" | custom-call | tf_op jit(solution)/shard_map/write/pallas_call | solution.py:474

commit v8 on v6

--- a/solution.py
+++ b/solution.py
@@ -419,7 +419,7 @@
         hidden = wg.shape[1]
         width = model // SUB
         block_rows = CAP * SUB
-        lane_chunks = [(low, min(512, width - low)) for low in range(0, width, 512)]
+        lane_chunks = [(0, width)]
         cuts = len(lane_chunks)
         anywhere = pl.BlockSpec(memory_space=pl.ANY)
         out = pl.pallas_call(

time: 32.5 us -> 32.5 us (level)
  no operation moved by 1% of the time
where the time goes in v8:
time: 32.5 us; the launch traced here: 32.4 us
  Pallas kernels  32.4 us (100%)
    pallas_call x1, Pallas kernels, body(): pl.pallas_call(functools.partial(kernel, (sections, ep), groups, lane_chu...  30.3 us
    pallas_call x1, Pallas kernels, body(): pl.pallas_call(write_kernel, out_shape=jax.ShapeDtypeStruct((tokens, mode...  2.04 us

profile of v8, /device:TPU:0, one launch (start us, length us, event | category | flops | bytes accessed | tf_op | source)
XLA Modules:
  0.0 32.4 jit_solution(400467489761459785)
XLA Ops:
  0.0 30.3 %experts.1.value_hbm = bf16[64,7168]{1,0:T(8,128)(2,1)} custom-call(bf16[64,7168]{1,0:T(8,128)(2,1)} %bitcast.16, bf16[64,7168]{1,0:T(8,128)(2,1)} %bitcast.17, s32[8,64]{1,0:T(8,128)} %bitcast.19, s32[8,64]{1,0:T(8,128)} %bitcast.20, f32[8,64]{1,0:T(8,128)} %bitcast.21, f32[8,64]{1,0:T(8,128)} %bitcast.22, f32[16,2,128]{2,1,0:T(2,128)} %bitcast.18, ...), custom_call_target="tpu_custom_call" | custom-call | tf_op jit(solution)/shard_map/experts/pallas_call | solution.py:425
  30.3 2.0 %write.1 = bf16[64,7168]{1,0:T(8,128)(2,1)} custom-call(bf16[64,7168]{1,0:T(8,128)(2,1)} %experts.1.value_hbm), custom_call_target="tpu_custom_call" | custom-call | tf_op jit(solution)/shard_map/write/pallas_call | solution.py:472
